TPU v7x, 32 devices: a whole 2x2x4 slice. The times are simulated.
32 devices in a mesh: parts: 2 (over x), blk: 16 (over z, y, core).
Axes of the slice: x: 2, y: 2, z: 4, core: 2. Of those that a mesh axis runs over, the one named last changes fastest.
Arguments:
- embeddings: bfloat16 [32768, 2048], P(('parts', 'blk')), parts along dimension 0, may hold values from -6 to 6
- projection: bfloat16 [4096, 64], P('parts'), parts along dimension 0, may hold values from -0.125 to 0.125
- loglen: float32 [128], P('parts'), parts along dimension 0, may hold values from 1.6 to 2.6
- left_solves: float32 [24, 32768], P(None, ('parts', 'blk')), parts along dimension 1, may hold values from -0.42426407 to 0.42426407
- right_solves: float32 [24, 32768], P(None, ('parts', 'blk')), parts along dimension 1, may hold values from -0.42426407 to 0.42426407
- assign: int32 [32768], P(('parts', 'blk')), parts along dimension 0, may hold values from 0 to 3
- plan: int32 [4, 32], P(None, ('parts', 'blk')), parts along dimension 1, may hold values from 0 to 65535
Outputs:
- projection_grad: float32 [4096, 64], P('parts'), parts along dimension 0
There are 2 independent parts, one for each index of `parts`. A program takes and returns all parts, laid end to end along the dimension named above; each array names one. Nothing has to cross between parts.
All inputs are finite; a program needn't handle non-finite values.
Results may differ from a plain program's by a relative error of at most 0.0031.
Values sent between devices are 32-bit elements; how exact they have to be, the bound alone decides.
No kernel may reach another device: no remote copies, remote signals or barrier semaphores. Data moves between devices by JAX's collectives and lax.ppermute only.
A program may use at most 128 MiB of HBM per device.

v0:
```python
import functools

import jax
import jax.numpy as jnp
from jax import lax
from jax.experimental import pallas as pl
from jax.experimental.pallas import tpu as pltpu
from jax.sharding import PartitionSpec as P

F = 64
C = 24
SUB = 4
STEPS = 4

LEFT = F
RIGHT = F + C
LABEL = F + 2 * C
PLAN = LABEL + 1
CORE = PLAN + STEPS
ROWS = 120

LOG2E = 1.4426950408889634
OFF = -1e30
CHUNK = 256
WIDE = 3 * F
NT = (((1,), (1,)), ((), ()))


def halves(value):
    hi = value.astype(jnp.bfloat16).astype(jnp.float32)
    return hi, value - hi


def thirds(value):
    hi, rest = halves(value)
    mid, low = halves(rest)
    return hi, mid, low


def own_operands(packet):
    points = packet.shape[1]
    z = packet[:F]
    hi, lo = halves(z * LOG2E)
    norm = jnp.sum(z * z, axis=0, keepdims=True) * (-0.5 * LOG2E)
    ones = jnp.ones((1, points), jnp.float32)
    labels = packet[LABEL : LABEL + 1]
    hot = [jnp.where(labels == float(u), 1.0, 0.0) for u in range(SUB)]
    tail = jnp.concatenate(list(thirds(norm)) + [ones] * 3 + hot + [jnp.zeros((54, points), jnp.float32)], axis=0)
    exponent = jnp.concatenate([hi, hi, lo, tail], axis=0)
    lh, ll = halves(packet[LEFT:RIGHT])
    rh, rl = halves(packet[RIGHT:LABEL])
    coupling = jnp.concatenate([lh, lh, ll, rh, rh, rl, jnp.zeros((256 - 6 * C, points), jnp.float32)], axis=0)
    return exponent, coupling


def bias_rows(plan, labels, ahead):
    sub = lax.broadcasted_iota(jnp.int32, (SUB, labels.shape[1]), 0)
    code = jnp.where(ahead, SUB * labels + sub, SUB * sub + labels)
    bit = jnp.bitwise_and(jnp.right_shift(jnp.broadcast_to(plan, code.shape), code), 1)
    return jnp.where(bit == 1, 0.0, OFF)


def visitor_operands(packet, bias, use_left=True, use_right=True):
    points = packet.shape[1]
    z = packet[:F]
    hi, lo = halves(z)
    norm = jnp.sum(z * z, axis=0, keepdims=True) * (-0.5 * LOG2E)
    ones = jnp.ones((1, points), jnp.float32)
    tail = jnp.concatenate([ones] * 3 + list(thirds(norm)) + [bias, jnp.zeros((54, points), jnp.float32)], axis=0)
    exponent = jnp.concatenate([hi, lo, hi, tail], axis=0)
    none = jnp.zeros((3 * C, points), jnp.float32)
    rh, rl = halves(packet[RIGHT:LABEL])
    lh, ll = halves(packet[LEFT:RIGHT])
    with_left = [rh, rl, rh] if use_left else [none]
    with_right = [lh, ll, lh] if use_right else [none]
    coupling = jnp.concatenate(with_left + with_right + [jnp.zeros((256 - 6 * C, points), jnp.float32)], axis=0)
    grads = jnp.concatenate([hi, jnp.ones((F, points), jnp.float32), lo], axis=0)
    return exponent.astype(jnp.bfloat16), coupling.astype(jnp.bfloat16), grads.astype(jnp.bfloat16)


def add_tile(acc_ref, own_exp_ref, own_cpl_ref, exp_ref, cpl_ref, grad_ref):
    points = own_exp_ref.shape[0]

    @pl.loop(0, points // CHUNK)
    def _(step):
        rows = pl.ds(pl.multiple_of(step * CHUNK, CHUNK), CHUNK)
        own_exp = own_exp_ref[rows, :]
        own_cpl = own_cpl_ref[rows, :]
        total = acc_ref[rows, :]
        for part in range(points // CHUNK):
            cols = slice(part * CHUNK, (part + 1) * CHUNK)
            power = jnp.dot(own_exp, exp_ref[:, cols], preferred_element_type=jnp.float32)
            couple = jnp.dot(own_cpl, cpl_ref[:, cols], preferred_element_type=jnp.float32)
            weights = jnp.exp2(power) * couple
            hi = weights.astype(jnp.bfloat16)
            lo = (weights - hi.astype(jnp.float32)).astype(jnp.bfloat16)
            grads = grad_ref[:, cols]
            total = total + lax.dot_general(hi, grads, NT, preferred_element_type=jnp.float32)
            total = total + lax.dot_general(lo, grads, NT, preferred_element_type=jnp.float32)
        acc_ref[rows, :] = total


def visit(packet, plan, ahead, slots, acc_ref, own_exp_ref, own_cpl_ref, **uses):
    exp_ref, cpl_ref, grad_ref = slots
    bias = bias_rows(plan, packet[LABEL : LABEL + 1].astype(jnp.int32), ahead)
    exp_ref[...], cpl_ref[...], grad_ref[...] = visitor_operands(packet, bias, **uses)
    add_tile(acc_ref, own_exp_ref, own_cpl_ref, exp_ref, cpl_ref, grad_ref)


def plan_of(packet, offset):
    return packet[PLAN + offset : PLAN + offset + 1].astype(jnp.int32)


def visit_at(own, packet, ahead, offset_first, offset_second, refs):
    second = own[CORE : CORE + 1] > 0.5
    is_ahead = jnp.where(second, ahead[1], ahead[0]) if ahead[0] != ahead[1] else jnp.full(second.shape, ahead[0])
    mine = jnp.where(second, plan_of(own, offset_second), plan_of(own, offset_first))
    theirs = jnp.where(second, plan_of(packet, offset_second), plan_of(packet, offset_first))
    plan = jnp.where(is_ahead, theirs, mine)
    acc_ref, own_exp_ref, own_cpl_ref, slots = refs
    visit(packet, plan, is_ahead, slots, acc_ref, own_exp_ref, own_cpl_ref)


def home_kernel(own_ref, acc_ref, own_exp_ref, own_cpl_ref, *slots):
    own = own_ref[...]
    exponent, coupling = own_operands(own)
    own_exp_ref[...] = exponent.T.astype(jnp.bfloat16)
    own_cpl_ref[...] = coupling.T.astype(jnp.bfloat16)
    acc_ref[...] = jnp.zeros_like(acc_ref)
    plan = plan_of(own, 0)
    behind = jnp.zeros(plan.shape, jnp.bool_)
    visit(own, plan, behind, slots, acc_ref, own_exp_ref, own_cpl_ref, use_right=False)
    visit(own, plan, ~behind, slots, acc_ref, own_exp_ref, own_cpl_ref, use_left=False)


def visit_kernel(places, *refs):
    n = len(places)
    own_ref, own_exp_ref, own_cpl_ref, before_ref = refs[:4]
    packets, acc_ref, slots = refs[4 : 4 + n], refs[4 + n], refs[5 + n :]
    acc_ref[...] = before_ref[...]
    own = own_ref[...]
    for packet_ref, (ahead, first, second) in zip(packets, places):
        visit_at(own, packet_ref[...], ahead, first, second, (acc_ref, own_exp_ref, own_cpl_ref, slots))


def slots_of(points):
    return [
        pltpu.VMEM((256, points), jnp.bfloat16),
        pltpu.VMEM((256, points), jnp.bfloat16),
        pltpu.VMEM((WIDE, points), jnp.bfloat16),
    ]


def cost(points, tiles):
    return pl.CostEstimate(
        flops=tiles * 8 * points * points * 256, bytes_accessed=1 << 20, transcendentals=tiles * points * points
    )


PARAMS = pltpu.CompilerParams(vmem_limit_bytes=40 << 20)


def home_tile(packet):
    points = packet.shape[1]
    return pl.pallas_call(
        home_kernel,
        out_shape=(
            jax.ShapeDtypeStruct((points, WIDE), jnp.float32),
            jax.ShapeDtypeStruct((points, 256), jnp.bfloat16),
            jax.ShapeDtypeStruct((points, 256), jnp.bfloat16),
        ),
        scratch_shapes=slots_of(points),
        cost_estimate=cost(points, 2),
        compiler_params=PARAMS,
        name="home_tile",
    )(packet)


def visitor_tiles(own, own_exp, own_cpl, acc, packets, places):
    points = own.shape[1]
    return pl.pallas_call(
        functools.partial(visit_kernel, places),
        out_shape=jax.ShapeDtypeStruct(acc.shape, jnp.float32),
        scratch_shapes=slots_of(points),
        cost_estimate=cost(points, len(places)),
        compiler_params=PARAMS,
        name="visitor_tiles",
    )(own, own_exp, own_cpl, acc, *packets)


def sent(value, target):
    count = lax.axis_size("blk")
    return lax.ppermute(value, "blk", [(source, target(source) % count) for source in range(count)])


def twin(value):
    return sent(value, lambda i: i ^ 1)


def sum_over_blk(term):
    count = lax.axis_size("blk")
    index = lax.axis_index("blk")
    second = (index % 2) == 1
    half = term.shape[0] // 2
    give = jnp.where(second, term[:half], term[half:])
    total = jnp.where(second, term[half:], term[:half]) + twin(give)
    spreads, unit = [], 4
    while unit < count:
        spread = min(4, count // unit)
        place = (index // unit) % spread
        if total.shape[0] % spread == 0:
            spreads.append((unit, spread, place))
            shares = total.reshape(spread, total.shape[0] // spread, total.shape[1])
            total = lax.dynamic_index_in_dim(shares, place, 0, False)
            for hop in range(spread - 1, 0, -1):
                passed = lax.dynamic_index_in_dim(shares, place ^ hop, 0, False)
                total = total + sent(passed, lambda i, step=unit * hop: i ^ step)
        else:
            for bit in range(1, spread.bit_length()):
                total = total + sent(total, lambda i, step=unit * bit: i ^ step)
        unit *= spread
    total = total + sent(total, lambda i: i ^ 2)
    for unit, spread, place in reversed(spreads):
        got = [total] + [sent(total, lambda i, step=unit * hop: i ^ step) for hop in range(1, spread)]
        got = jnp.stack(got)
        total = jnp.concatenate([lax.dynamic_index_in_dim(got, place ^ at, 0, False) for at in range(spread)])
    other = twin(total)
    return jnp.where(second, jnp.concatenate([other, total]), jnp.concatenate([total, other]))


def project(embeddings, projection, loglen):
    inverse_len = jnp.exp(-loglen)
    features = lax.dot_general(
        projection, embeddings, (((0,), (1,)), ((), ())), preferred_element_type=jnp.float32
    )
    return (features * inverse_len[:, None], inverse_len)


def per_device(embeddings, projection, loglen, left_solves, right_solves, assign, plan):
    points = embeddings.shape[0]
    features, inverse_len = project(embeddings, projection, loglen)
    core = lax.axis_index("blk") % 2
    rest = jnp.concatenate(
        [
            assign[None, :].astype(jnp.float32),
            jnp.broadcast_to(plan.astype(jnp.float32), (STEPS, points)),
            jnp.broadcast_to(core.astype(jnp.float32), (1, points)),
            jnp.zeros((ROWS - CORE - 1, points), jnp.float32),
        ],
        axis=0,
    )
    own = jnp.concatenate([features, left_solves, right_solves, rest], axis=0)
    near = twin(own)
    down = sent(own, lambda i: i + 2)
    up = sent(own, lambda i: i - 2)
    far = sent(own, lambda i: i + 3 if i % 2 else i - 3)
    acc, own_exp, own_cpl = home_tile(own)
    tiles = functools.partial(visitor_tiles, own, own_exp, own_cpl)
    acc = tiles(acc, [near], [((True, False), 1, 1)])
    acc = tiles(acc, [down, twin(down)], [((False, False), 2, 2), ((False, False), 1, 3)])
    acc = tiles(acc, [far], [((False, True), 3, 3)])
    acc = tiles(acc, [up, twin(up)], [((True, True), 2, 2), ((True, True), 3, 1)])
    grad_z = (acc[:, :F] + acc[:, 2 * F :]).T - features * acc[:, F : 2 * F].T
    grad_x = (grad_z * inverse_len[:, None]).astype(jnp.bfloat16)
    local_term = lax.dot_general(
        grad_x, embeddings, (((1,), (0,)), ((), ())), preferred_element_type=jnp.float32
    )
    return sum_over_blk(local_term).T


def solution(mesh):
    return jax.shard_map(
        per_device,
        mesh=mesh,
        in_specs=(
            P(("parts", "blk"), None),
            P("parts", None),
            P("parts"),
            P(None, ("parts", "blk")),
            P(None, ("parts", "blk")),
            P(("parts", "blk")),
            P(None, ("parts", "blk")),
        ),
        out_specs=P("parts", None),
        check_vma=False,
    )
```

profile of v0, /device:TPU:0, one launch (start us, length us, event | category | flops | bytes accessed | tf_op | source)
XLA Modules:
  0.0 95.1 jit_solution(17071398735290343206)
XLA Ops:
  0.0 0.7 negate_exponential_fusion
  0.7 0.7 convert_bitcast_fusion
  1.4 0.7 convert_element_type.15
  2.1 0.0 copy-done
  2.1 3.6 %convolution_multiply_fusion = f32[64,1024]{1,0:T(8,128)S(1)} fusion(bf16[2048,64]{0,1:T(8,128)(2,1)S(1)} %copy-done, bf16[1024,2048]{1,0:T(8,128)(2,1)} %param.7, f32[64]{0:T(128)S(1)} %negate_exponential_fusion), kind=kOutput, calls=%fused_computation | convolution fusion | flops 268500992 | bytes 4718848 | tf_op jit(solution)/shard_map/dot_general | solution.py:233
  5.7 0.1 broadcast_in_dim.17
  5.8 0.1 concatenate.14.own_ref.refs_0_
  5.8 3.0 %collective-permute-start.1 = (f32[120,1024]{1,0:T(8,128)S(1)}, f32[120,1024]{1,0:T(8,128)S(1)}, u32[]{:S(2)}, u32[]{:S(2)}) collective-permute-start(f32[120,1024]{1,0:T(8,128)S(1)} %concatenate.14.own_ref.refs_0_), channel_id=1, source_target_pairs={{0,2},{1,3},{2,4},{3,5},{4,6},{5,7},{6,8},{7,9},{8,10},{9,11},{10,... | collective-permute-start | bytes 1474568 | tf_op jit(solution)/shard_map/ppermute | solution.py:193
  8.9 3.1 %collective-permute-start.4 = (f32[120,1024]{1,0:T(8,128)S(1)}, f32[120,1024]{1,0:T(8,128)S(1)}, u32[]{:S(2)}, u32[]{:S(2)}) collective-permute-start(f32[120,1024]{1,0:T(8,128)S(1)} %concatenate.14.own_ref.refs_0_), channel_id=1, source_target_pairs={{0,14},{1,15},{2,0},{3,1},{4,2},{5,3},{6,4},{7,5},{8,6},{9,7},{10,... | collective-permute-start | bytes 1474568 | tf_op jit(solution)/shard_map/ppermute | solution.py:193
  12.0 0.0 collective-permute-start
  12.0 2.0 %collective-permute-start.3 = (f32[120,1024]{1,0:T(8,128)S(1)}, f32[120,1024]{1,0:T(8,128)S(1)}, u32[]{:S(2)}, u32[]{:S(2)}) collective-permute-start(f32[120,1024]{1,0:T(8,128)S(1)} %concatenate.14.own_ref.refs_0_), channel_id=1, source_target_pairs={{0,13},{1,4},{2,15},{3,6},{4,1},{5,8},{6,3},{7,10},{8,5},{9,12},{1... | collective-permute-start | bytes 1474568 | tf_op jit(solution)/shard_map/ppermute | solution.py:193
  14.0 15.9 %collective-permute-done.1.refs_4_ = f32[120,1024]{1,0:T(8,128)S(1)} collective-permute-done((f32[120,1024]{1,0:T(8,128)S(1)}, f32[120,1024]{1,0:T(8,128)S(1)}, u32[]{:S(2)}, u32[]{:S(2)}) %collective-permute-start.1) | collective-permute-done | bytes 491552 | tf_op jit(solution)/shard_map/ppermute | solution.py:193
  29.9 0.0 collective-permute-start.2
  29.9 8.4 %home_tile.1 = (f32[1024,192]{1,0:T(8,128)S(1)}, bf16[1024,256]{1,0:T(8,128)(2,1)S(1)}, bf16[1024,256]{1,0:T(8,128)(2,1)S(1)}) custom-call(f32[120,1024]{1,0:T(8,128)S(1)} %concatenate.14.own_ref.refs_0_), custom_call_target="tpu_custom_call" | custom-call | flops 4294967296 | bytes 1048576 | tf_op jit(solution)/shard_map/home_tile/pallas_call | solution.py:165
  38.2 0.0 collective-permute-done.4.refs_4_
  38.2 0.6 collective-permute-start.5
  38.8 0.0 collective-permute-done.refs_4_
  38.8 4.1 %visitor_tiles.4.refs_3_ = f32[1024,192]{1,0:T(8,128)S(1)} custom-call(f32[120,1024]{1,0:T(8,128)S(1)} %concatenate.14.own_ref.refs_0_, bf16[1024,256]{1,0:T(8,128)(2,1)S(1)} %get-tuple-element.8.refs_1_, bf16[1024,256]{1,0:T(8,128)(2,1)S(1)} %get-tuple-element.9.refs_2_, f32[1024,192]{1,0:T(8,128)S(1)} %get-tuple-element.10.refs_3_, ...), custom_call_target="tpu_custom_call" | custom-call | flops 2147483648 | bytes 1048576 | tf_op jit(solution)/shard_map/visitor_tiles/pallas_call | solution.py:181
  42.9 0.0 collective-permute-done.2.refs_5_
  42.9 8.1 %visitor_tiles.5.refs_3_ = f32[1024,192]{1,0:T(8,128)S(1)} custom-call(f32[120,1024]{1,0:T(8,128)S(1)} %concatenate.14.own_ref.refs_0_, bf16[1024,256]{1,0:T(8,128)(2,1)S(1)} %get-tuple-element.8.refs_1_, bf16[1024,256]{1,0:T(8,128)(2,1)S(1)} %get-tuple-element.9.refs_2_, f32[1024,192]{1,0:T(8,128)S(1)} %visitor_tiles.4.refs_3_, ...), custom_call_target="tpu_custom_call" | custom-call | flops 4294967296 | bytes 1048576 | tf_op jit(solution)/shard_map/visitor_tiles/pallas_call | solution.py:181
  51.0 0.0 collective-permute-done.3.refs_4_
  51.1 4.1 %visitor_tiles.6.refs_3_ = f32[1024,192]{1,0:T(8,128)S(1)} custom-call(f32[120,1024]{1,0:T(8,128)S(1)} %concatenate.14.own_ref.refs_0_, bf16[1024,256]{1,0:T(8,128)(2,1)S(1)} %get-tuple-element.8.refs_1_, bf16[1024,256]{1,0:T(8,128)(2,1)S(1)} %get-tuple-element.9.refs_2_, f32[1024,192]{1,0:T(8,128)S(1)} %visitor_tiles.5.refs_3_, ...), custom_call_target="tpu_custom_call" | custom-call | flops 2147483648 | bytes 1048576 | tf_op jit(solution)/shard_map/visitor_tiles/pallas_call | solution.py:181
  55.2 0.0 collective-permute-done.5.refs_5_
  55.2 8.1 %visitor_tiles.7 = f32[1024,192]{1,0:T(8,128)S(1)} custom-call(f32[120,1024]{1,0:T(8,128)S(1)} %concatenate.14.own_ref.refs_0_, bf16[1024,256]{1,0:T(8,128)(2,1)S(1)} %get-tuple-element.8.refs_1_, bf16[1024,256]{1,0:T(8,128)(2,1)S(1)} %get-tuple-element.9.refs_2_, f32[1024,192]{1,0:T(8,128)S(1)} %visitor_tiles.6.refs_3_, ...), custom_call_target="tpu_custom_call" | custom-call | flops 4294967296 | bytes 1048576 | tf_op jit(solution)/shard_map/visitor_tiles/pallas_call | solution.py:181
  63.3 0.2 fusion.8
  63.5 0.2 copy.11
  63.7 0.2 copy.12
  63.8 0.2 copy.13
  64.0 3.1 %fusion.3 = f32[64,2048]{1,0:T(8,128)S(1)} fusion(bf16[1024,2048]{1,0:T(8,128)(2,1)} %param.7, f32[64,1024]{1,0:T(8,128)S(1)} %convolution_multiply_fusion, f32[1024,64]{0,1:T(8,128)S(1)} %copy.13, f32[1024,64]{0,1:T(8,128)S(1)} %copy.11, f32[1024,64]{0,1:T(8,128)S(1)} %copy.12, f32[64]{0:T(128)S(1)} %negate_exponential_fusion), kind=kOutput, calls=%fused_computation.10 | convolution fusion | flops 268763136 | bytes 5767424 | tf_op jit(solution)/shard_map/dot_general | solution.py:265
  67.2 0.1 collective-permute-start.6
  67.3 1.5 %collective-permute-done.6 = f32[32,2048]{1,0:T(8,128)S(1)} collective-permute-done((f32[32,2048]{1,0:T(8,128)S(1)}, f32[32,2048]{1,0:T(8,128)S(1)}, u32[]{:S(2)}, u32[]{:S(2)}) %collective-permute-start.6) | collective-permute-done | bytes 262176 | tf_op jit(solution)/shard_map/ppermute | solution.py:193
  68.8 3.7 %collective-permute-start.7 = (f32[8,2048]{1,0:T(8,128)S(1)}, f32[8,2048]{1,0:T(8,128)S(1)}, u32[]{:S(2)}, u32[]{:S(2)}) collective-permute-start(f32[8,2048]{1,0:T(8,128)S(1)} %get-tuple-element.24), channel_id=1, source_target_pairs={{0,12},{1,13},{2,14},{3,15},{4,8},{5,9},{6,10},{7,11},{8,4},{9,5},... | collective-permute-start | bytes 196616 | tf_op jit(solution)/shard_map/ppermute | solution.py:193
  72.5 0.0 collective-permute-start.8
  72.5 0.8 collective-permute-start.9
  73.3 1.9 %collective-permute-done.7 = f32[8,2048]{1,0:T(8,128)S(1)} collective-permute-done((f32[8,2048]{1,0:T(8,128)S(1)}, f32[8,2048]{1,0:T(8,128)S(1)}, u32[]{:S(2)}, u32[]{:S(2)}) %collective-permute-start.7) | collective-permute-done | bytes 65568 | tf_op jit(solution)/shard_map/ppermute | solution.py:193
  75.2 3.2 %collective-permute-done.8 = f32[8,2048]{1,0:T(8,128)S(1)} collective-permute-done((f32[8,2048]{1,0:T(8,128)S(1)}, f32[8,2048]{1,0:T(8,128)S(1)}, u32[]{:S(2)}, u32[]{:S(2)}) %collective-permute-start.8) | collective-permute-done | bytes 65568 | tf_op jit(solution)/shard_map/ppermute | solution.py:193
  78.4 0.0 collective-permute-done.9
  78.4 2.6 %collective-permute-start.10 = (f32[8,2048]{1,0:T(8,128)S(1)}, f32[8,2048]{1,0:T(8,128)S(1)}, u32[]{:S(2)}, u32[]{:S(2)}) collective-permute-start(f32[8,2048]{1,0:T(8,128)S(1)} %fusion.7), channel_id=1, source_target_pairs={{0,2},{1,3},{2,0},{3,1},{4,6},{5,7},{6,4},{7,5},{8,10},{9,11},{10,... | collective-permute-start | bytes 196616 | tf_op jit(solution)/shard_map/ppermute | solution.py:193
  81.0 2.2 %collective-permute-done.10 = f32[8,2048]{1,0:T(8,128)S(1)} collective-permute-done((f32[8,2048]{1,0:T(8,128)S(1)}, f32[8,2048]{1,0:T(8,128)S(1)}, u32[]{:S(2)}, u32[]{:S(2)}) %collective-permute-start.10) | collective-permute-done | bytes 65568 | tf_op jit(solution)/shard_map/ppermute | solution.py:193
  83.2 1.2 %collective-permute-start.11 = (f32[8,2048]{1,0:T(8,128)S(1)}, f32[8,2048]{1,0:T(8,128)S(1)}, u32[]{:S(2)}, u32[]{:S(2)}) collective-permute-start(f32[8,2048]{1,0:T(8,128)S(1)} %add.55), channel_id=1, source_target_pairs={{0,4},{1,5},{2,6},{3,7},{4,0},{5,1},{6,2},{7,3},{8,12},{9,13},{10,... | collective-permute-start | bytes 196616 | tf_op jit(solution)/shard_map/ppermute | solution.py:193
  84.4 1.9 %collective-permute-start.12 = (f32[8,2048]{1,0:T(8,128)S(1)}, f32[8,2048]{1,0:T(8,128)S(1)}, u32[]{:S(2)}, u32[]{:S(2)}) collective-permute-start(f32[8,2048]{1,0:T(8,128)S(1)} %add.55), channel_id=1, source_target_pairs={{0,8},{1,9},{2,10},{3,11},{4,12},{5,13},{6,14},{7,15},{8,0},{9,1},... | collective-permute-start | bytes 196616 | tf_op jit(solution)/shard_map/ppermute | solution.py:193
  86.3 1.3 %collective-permute-start.13 = (f32[8,2048]{1,0:T(8,128)S(1)}, f32[8,2048]{1,0:T(8,128)S(1)}, u32[]{:S(2)}, u32[]{:S(2)}) collective-permute-start(f32[8,2048]{1,0:T(8,128)S(1)} %add.55), channel_id=1, source_target_pairs={{0,12},{1,13},{2,14},{3,15},{4,8},{5,9},{6,10},{7,11},{8,4},{9,5},... | collective-permute-start | bytes 196616 | tf_op jit(solution)/shard_map/ppermute | solution.py:193
  87.7 0.0 collective-permute-done.11
  87.7 3.1 %collective-permute-done.12 = f32[8,2048]{1,0:T(8,128)S(1)} collective-permute-done((f32[8,2048]{1,0:T(8,128)S(1)}, f32[8,2048]{1,0:T(8,128)S(1)}, u32[]{:S(2)}, u32[]{:S(2)}) %collective-permute-start.12) | collective-permute-done | bytes 65568 | tf_op jit(solution)/shard_map/ppermute | solution.py:193
  90.8 1.6 %collective-permute-done.13 = f32[8,2048]{1,0:T(8,128)S(1)} collective-permute-done((f32[8,2048]{1,0:T(8,128)S(1)}, f32[8,2048]{1,0:T(8,128)S(1)}, u32[]{:S(2)}, u32[]{:S(2)}) %collective-permute-start.13) | collective-permute-done | bytes 65568 | tf_op jit(solution)/shard_map/ppermute | solution.py:193
  92.6 0.1 collective-permute-start.14
  92.6 1.5 %collective-permute-done.14 = f32[32,2048]{1,0:T(8,128)S(1)} collective-permute-done((f32[32,2048]{1,0:T(8,128)S(1)}, f32[32,2048]{1,0:T(8,128)S(1)}, u32[]{:S(2)}, u32[]{:S(2)}) %collective-permute-start.14) | collective-permute-done | bytes 262176 | tf_op jit(solution)/shard_map/ppermute | solution.py:193
  94.3 0.9 select_bitcast_fusion
  (23 shorter events, 0.3 us)
Async XLA Ops:
  0.0 2.1 %copy-start = (bf16[2048,64]{0,1:T(8,128)(2,1)S(1)}, bf16[2048,64]{0,1:T(8,128)(2,1)}, u32[]{:S(2)}) copy-start(bf16[2048,64]{0,1:T(8,128)(2,1)} %param.8) | copy-start | bytes 786436
  0.0 5.7 %copy-start.1 = (f32[24,1024]{1,0:T(8,128)S(1)}, f32[24,1024]{1,0:T(8,128)}, u32[]{:S(2)}) copy-start(f32[24,1024]{1,0:T(8,128)} %param.10) | copy-start | bytes 294916
  0.0 5.7 %copy-start.2 = (f32[24,1024]{1,0:T(8,128)S(1)}, f32[24,1024]{1,0:T(8,128)}, u32[]{:S(2)}) copy-start(f32[24,1024]{1,0:T(8,128)} %param.11) | copy-start | bytes 294916
  5.8 24.0 %collective-permute-start.1 = (f32[120,1024]{1,0:T(8,128)S(1)}, f32[120,1024]{1,0:T(8,128)S(1)}, u32[]{:S(2)}, u32[]{:S(2)}) collective-permute-start(f32[120,1024]{1,0:T(8,128)S(1)} %concatenate.14.own_ref.refs_0_), channel_id=1, source_target_pairs={{0,2},{1,3},{2,4},{3,5},{4,6},{5,7},{6,8},{7,9},{8,10},{9,11},{10,... | collective-permute-start | bytes 1474568 | tf_op jit(solution)/shard_map/ppermute | solution.py:193
  8.9 29.4 %collective-permute-start.4 = (f32[120,1024]{1,0:T(8,128)S(1)}, f32[120,1024]{1,0:T(8,128)S(1)}, u32[]{:S(2)}, u32[]{:S(2)}) collective-permute-start(f32[120,1024]{1,0:T(8,128)S(1)} %concatenate.14.own_ref.refs_0_), channel_id=1, source_target_pairs={{0,14},{1,15},{2,0},{3,1},{4,2},{5,3},{6,4},{7,5},{8,6},{9,7},{10,... | collective-permute-start | bytes 1474568 | tf_op jit(solution)/shard_map/ppermute | solution.py:193
  12.0 26.9 %collective-permute-start = (f32[120,1024]{1,0:T(8,128)S(1)}, f32[120,1024]{1,0:T(8,128)S(1)}, u32[]{:S(2)}, u32[]{:S(2)}) collective-permute-start(f32[120,1024]{1,0:T(8,128)S(1)} %concatenate.14.own_ref.refs_0_), channel_id=1, source_target_pairs={{0,1},{1,0},{2,3},{3,2},{4,5},{5,4},{6,7},{7,6},{8,9},{9,8},{10,11... | collective-permute-start | bytes 1474568 | tf_op jit(solution)/shard_map/ppermute | solution.py:193
  12.0 39.1 %collective-permute-start.3 = (f32[120,1024]{1,0:T(8,128)S(1)}, f32[120,1024]{1,0:T(8,128)S(1)}, u32[]{:S(2)}, u32[]{:S(2)}) collective-permute-start(f32[120,1024]{1,0:T(8,128)S(1)} %concatenate.14.own_ref.refs_0_), channel_id=1, source_target_pairs={{0,13},{1,4},{2,15},{3,6},{4,1},{5,8},{6,3},{7,10},{8,5},{9,12},{1... | collective-permute-start | bytes 1474568 | tf_op jit(solution)/shard_map/ppermute | solution.py:193
  29.9 13.1 %collective-permute-start.2 = (f32[120,1024]{1,0:T(8,128)S(1)}, f32[120,1024]{1,0:T(8,128)S(1)}, u32[]{:S(2)}, u32[]{:S(2)}) collective-permute-start(f32[120,1024]{1,0:T(8,128)S(1)} %collective-permute-done.1.refs_4_), channel_id=1, source_target_pairs={{0,1},{1,0},{2,3},{3,2},{4,5},{5,4},{6,7},{7,6},{8,9},{9,8},{10,11... | collective-permute-start | bytes 1474568 | tf_op jit(solution)/shard_map/ppermute | solution.py:193
  38.2 16.9 %collective-permute-start.5 = (f32[120,1024]{1,0:T(8,128)S(1)}, f32[120,1024]{1,0:T(8,128)S(1)}, u32[]{:S(2)}, u32[]{:S(2)}) collective-permute-start(f32[120,1024]{1,0:T(8,128)S(1)} %collective-permute-done.4.refs_4_), channel_id=1, source_target_pairs={{0,1},{1,0},{2,3},{3,2},{4,5},{5,4},{6,7},{7,6},{8,9},{9,8},{10,11... | collective-permute-start | bytes 1474568 | tf_op jit(solution)/shard_map/ppermute | solution.py:193
  67.2 1.6 %collective-permute-start.6 = (f32[32,2048]{1,0:T(8,128)S(1)}, f32[32,2048]{1,0:T(8,128)S(1)}, u32[]{:S(2)}, u32[]{:S(2)}) collective-permute-start(f32[32,2048]{1,0:T(8,128)S(1)} %slice_select_fusion), channel_id=1, source_target_pairs={{0,1},{1,0},{2,3},{3,2},{4,5},{5,4},{6,7},{7,6},{8,9},{9,8},{10,11... | collective-permute-start | bytes 786440 | tf_op jit(solution)/shard_map/ppermute | solution.py:193
  68.8 6.4 %collective-permute-start.7 = (f32[8,2048]{1,0:T(8,128)S(1)}, f32[8,2048]{1,0:T(8,128)S(1)}, u32[]{:S(2)}, u32[]{:S(2)}) collective-permute-start(f32[8,2048]{1,0:T(8,128)S(1)} %get-tuple-element.24), channel_id=1, source_target_pairs={{0,12},{1,13},{2,14},{3,15},{4,8},{5,9},{6,10},{7,11},{8,4},{9,5},... | collective-permute-start | bytes 196616 | tf_op jit(solution)/shard_map/ppermute | solution.py:193
  72.5 5.9 %collective-permute-start.8 = (f32[8,2048]{1,0:T(8,128)S(1)}, f32[8,2048]{1,0:T(8,128)S(1)}, u32[]{:S(2)}, u32[]{:S(2)}) collective-permute-start(f32[8,2048]{1,0:T(8,128)S(1)} %get-tuple-element.26), channel_id=1, source_target_pairs={{0,8},{1,9},{2,10},{3,11},{4,12},{5,13},{6,14},{7,15},{8,0},{9,1},... | collective-permute-start | bytes 196616 | tf_op jit(solution)/shard_map/ppermute | solution.py:193
  72.5 5.9 %collective-permute-start.9 = (f32[8,2048]{1,0:T(8,128)S(1)}, f32[8,2048]{1,0:T(8,128)S(1)}, u32[]{:S(2)}, u32[]{:S(2)}) collective-permute-start(f32[8,2048]{1,0:T(8,128)S(1)} %get-tuple-element.25), channel_id=1, source_target_pairs={{0,4},{1,5},{2,6},{3,7},{4,0},{5,1},{6,2},{7,3},{8,12},{9,13},{10,... | collective-permute-start | bytes 196616 | tf_op jit(solution)/shard_map/ppermute | solution.py:193
  78.4 4.8 %collective-permute-start.10 = (f32[8,2048]{1,0:T(8,128)S(1)}, f32[8,2048]{1,0:T(8,128)S(1)}, u32[]{:S(2)}, u32[]{:S(2)}) collective-permute-start(f32[8,2048]{1,0:T(8,128)S(1)} %fusion.7), channel_id=1, source_target_pairs={{0,2},{1,3},{2,0},{3,1},{4,6},{5,7},{6,4},{7,5},{8,10},{9,11},{10,... | collective-permute-start | bytes 196616 | tf_op jit(solution)/shard_map/ppermute | solution.py:193
  83.2 4.5 %collective-permute-start.11 = (f32[8,2048]{1,0:T(8,128)S(1)}, f32[8,2048]{1,0:T(8,128)S(1)}, u32[]{:S(2)}, u32[]{:S(2)}) collective-permute-start(f32[8,2048]{1,0:T(8,128)S(1)} %add.55), channel_id=1, source_target_pairs={{0,4},{1,5},{2,6},{3,7},{4,0},{5,1},{6,2},{7,3},{8,12},{9,13},{10,... | collective-permute-start | bytes 196616 | tf_op jit(solution)/shard_map/ppermute | solution.py:193
  84.4 6.4 %collective-permute-start.12 = (f32[8,2048]{1,0:T(8,128)S(1)}, f32[8,2048]{1,0:T(8,128)S(1)}, u32[]{:S(2)}, u32[]{:S(2)}) collective-permute-start(f32[8,2048]{1,0:T(8,128)S(1)} %add.55), channel_id=1, source_target_pairs={{0,8},{1,9},{2,10},{3,11},{4,12},{5,13},{6,14},{7,15},{8,0},{9,1},... | collective-permute-start | bytes 196616 | tf_op jit(solution)/shard_map/ppermute | solution.py:193
  86.3 6.1 %collective-permute-start.13 = (f32[8,2048]{1,0:T(8,128)S(1)}, f32[8,2048]{1,0:T(8,128)S(1)}, u32[]{:S(2)}, u32[]{:S(2)}) collective-permute-start(f32[8,2048]{1,0:T(8,128)S(1)} %add.55), channel_id=1, source_target_pairs={{0,12},{1,13},{2,14},{3,15},{4,8},{5,9},{6,10},{7,11},{8,4},{9,5},... | collective-permute-start | bytes 196616 | tf_op jit(solution)/shard_map/ppermute | solution.py:193
  92.6 1.6 %collective-permute-start.14 = (f32[32,2048]{1,0:T(8,128)S(1)}, f32[32,2048]{1,0:T(8,128)S(1)}, u32[]{:S(2)}, u32[]{:S(2)}) collective-permute-start(f32[32,2048]{1,0:T(8,128)S(1)} %pad_maximum_fusion.1), channel_id=1, source_target_pairs={{0,1},{1,0},{2,3},{3,2},{4,5},{5,4},{6,7},{7,6},{8,9},{9,8},{10,11... | collective-permute-start | bytes 786440 | tf_op jit(solution)/shard_map/ppermute | solution.py:193
where the time goes:
time: 95.4 us; the launch traced here: 95.1 us
  Pallas kernels  32.7 us (34%)
  waiting for transfers between devices  31 us (32%)
  starting transfers between devices  20.3 us (21%)
  matrix products  6.67 us (7%)
  other arithmetic  3.05 us (3%)
  local copies, waits for them, and re-layouts  1.06 us (1%)
    ppermute x15, waiting for transfers between devices, sent(): lax.ppermute(value, 'blk', [(source, target(source) % count) for source i...  31 us
    pallas_call x4, Pallas kernels, visitor_tiles(): pl.pallas_call(functools.partial(visit_kernel, places), out_shape=jax.Sha...  24.4 us
    ppermute x15, starting transfers between devices, sent(): lax.ppermute(value, 'blk', [(source, target(source) % count) for source i...  20.3 us
    pallas_call x1, Pallas kernels, home_tile(): pl.pallas_call(home_kernel, out_shape=(jax.ShapeDtypeStruct((points, WIDE...  8.35 us
    dot_general x1, matrix products, project(): lax.dot_general(projection, embeddings, (((0,), (1,)), ((), ())), preferr...  3.58 us
    dot_general x1, matrix products, per_device(): lax.dot_general(grad_x, embeddings, (((1,), (0,)), ((), ())), preferred_e...  3.09 us
  transfers between devices with their start and end apart: 15, of which 8 were waited for; matrix products, arithmetic and copies ran while one was open for 0% of the time, Pallas kernels for 26%

commit v1 on v0

v1 whole, which is shorter than its diff:
```python
import functools

import jax
import jax.numpy as jnp
from jax import lax
from jax.experimental import pallas as pl
from jax.experimental.pallas import tpu as pltpu
from jax.sharding import PartitionSpec as P

F = 64
C = 24
SUB = 4
STEPS = 4

LEFT = F
RIGHT = F + C
LABEL = F + 2 * C
PLAN = LABEL + 1
CORE = PLAN + STEPS
ROWS = 120

LOG2E = 1.4426950408889634
OFF = -1e30
CHUNK = 512
PIECES = 8
WIDE = 3 * F
FAR = ((False, 3), (True, 3))
NT = (((1,), (1,)), ((), ()))


def halves(value):
    hi = value.astype(jnp.bfloat16).astype(jnp.float32)
    return hi, value - hi


def thirds(value):
    hi, rest = halves(value)
    mid, low = halves(rest)
    return hi, mid, low


def own_operands(packet):
    points = packet.shape[1]
    z = packet[:F]
    hi, lo = halves(z * LOG2E)
    norm = jnp.sum(z * z, axis=0, keepdims=True) * (-0.5 * LOG2E)
    ones = jnp.ones((1, points), jnp.float32)
    labels = packet[LABEL : LABEL + 1]
    hot = [jnp.where(labels == float(u), 1.0, 0.0) for u in range(SUB)]
    tail = jnp.concatenate(list(thirds(norm)) + [ones] * 3 + hot + [jnp.zeros((54, points), jnp.float32)], axis=0)
    exponent = jnp.concatenate([hi, hi, lo, tail], axis=0)
    lh, ll = halves(packet[LEFT:RIGHT])
    rh, rl = halves(packet[RIGHT:LABEL])
    coupling = jnp.concatenate([lh, lh, ll, rh, rh, rl, jnp.zeros((256 - 6 * C, points), jnp.float32)], axis=0)
    return exponent, coupling


def bias_rows(plan, labels, ahead):
    sub = lax.broadcasted_iota(jnp.int32, (SUB, labels.shape[1]), 0)
    code = jnp.where(ahead, SUB * labels + sub, SUB * sub + labels)
    bit = jnp.bitwise_and(jnp.right_shift(jnp.broadcast_to(plan, code.shape), code), 1)
    return jnp.where(bit == 1, 0.0, OFF)


def gradient_rows(hi, lo):
    return jnp.concatenate([hi, jnp.ones_like(hi), lo], axis=0)


def visitor_operands(packet, bias, use_left=True, use_right=True):
    points = packet.shape[1]
    z = packet[:F]
    hi, lo = halves(z)
    norm = jnp.sum(z * z, axis=0, keepdims=True) * (-0.5 * LOG2E)
    ones = jnp.ones((1, points), jnp.float32)
    tail = jnp.concatenate([ones] * 3 + list(thirds(norm)) + [bias, jnp.zeros((54, points), jnp.float32)], axis=0)
    exponent = jnp.concatenate([hi, lo, hi, tail], axis=0)
    none = jnp.zeros((3 * C, points), jnp.float32)
    rh, rl = halves(packet[RIGHT:LABEL])
    lh, ll = halves(packet[LEFT:RIGHT])
    with_left = [rh, rl, rh] if use_left else [none]
    with_right = [lh, ll, lh] if use_right else [none]
    coupling = jnp.concatenate(with_left + with_right + [jnp.zeros((256 - 6 * C, points), jnp.float32)], axis=0)
    grads = gradient_rows(hi, lo)
    return exponent.astype(jnp.bfloat16), coupling.astype(jnp.bfloat16), grads.astype(jnp.bfloat16)


def add_tile(acc_ref, before_ref, home_exp_ref, home_cpl_ref, slots, back=None):
    exp_ref, cpl_ref, grad_ref = slots
    points, visitors = home_exp_ref.shape[0], exp_ref.shape[1]
    for row in range(0, points, CHUNK):
        rows = slice(row, row + CHUNK)
        home_exp, home_cpl = home_exp_ref[rows, :], home_cpl_ref[rows, :]
        total = None if before_ref is None else before_ref[rows, :]
        for col in range(0, visitors, CHUNK):
            cols = slice(col, col + CHUNK)
            power = jnp.dot(home_exp, exp_ref[:, cols], preferred_element_type=jnp.float32)
            couple = jnp.dot(home_cpl, cpl_ref[:, cols], preferred_element_type=jnp.float32)
            weights = jnp.exp2(power) * couple
            hi = weights.astype(jnp.bfloat16)
            lo = (weights - hi.astype(jnp.float32)).astype(jnp.bfloat16)
            for part in (hi, lo):
                term = lax.dot_general(part, grad_ref[:, cols], NT, preferred_element_type=jnp.float32)
                total = term if total is None else total + term
            if back is not None:
                back_ref, home_rows_ref, fresh = back
                term = jnp.dot(home_rows_ref[:, rows], hi, preferred_element_type=jnp.float32)
                term += jnp.dot(home_rows_ref[:, rows], lo, preferred_element_type=jnp.float32)
                back_ref[:, cols] = term if fresh and row == 0 else back_ref[:, cols] + term
        acc_ref[rows, :] = total


def visit(packet, plan, ahead, slots, acc_ref, before_ref, home_exp_ref, home_cpl_ref, back=None, **uses):
    exp_ref, cpl_ref, grad_ref = slots
    bias = bias_rows(plan, packet[LABEL : LABEL + 1].astype(jnp.int32), ahead)
    exp_ref[...], cpl_ref[...], grad_ref[...] = visitor_operands(packet, bias, **uses)
    add_tile(acc_ref, before_ref, home_exp_ref, home_cpl_ref, slots, back)


def plan_of(packet, offset):
    return packet[PLAN + offset : PLAN + offset + 1].astype(jnp.int32)


def visit_at(second, home, packet, place, acc_ref, before_ref, factors, slots, back=None):
    (ahead_first, offset_first), (ahead_second, offset_second) = place
    ahead = jnp.logical_or(jnp.logical_and(second, ahead_second), jnp.logical_and(~second, ahead_first))
    mine = jnp.where(second, plan_of(home, offset_second), plan_of(home, offset_first))
    theirs = jnp.where(second, plan_of(packet, offset_second), plan_of(packet, offset_first))
    plan = jnp.where(ahead, theirs, mine)
    visit(packet, plan, ahead, slots, acc_ref, before_ref, *factors, back=back)


def prepare(packet, exp_ref, cpl_ref, rows_ref):
    exponent, coupling = own_operands(packet)
    exp_ref[...] = exponent.T.astype(jnp.bfloat16)
    cpl_ref[...] = coupling.T.astype(jnp.bfloat16)
    rows_ref[...] = gradient_rows(*halves(packet[:F])).astype(jnp.bfloat16)


def is_second(own_ref):
    return own_ref[CORE : CORE + 1, :] > 0.5


def home_kernel(own_ref, acc_ref, exp_ref, cpl_ref, rows_ref, again_ref, *slots):
    own = own_ref[...]
    again_ref[...] = own
    prepare(own, exp_ref, cpl_ref, rows_ref)
    plan = plan_of(own, 0)
    behind = jnp.zeros(plan.shape, jnp.bool_)
    visit(own, plan, behind, slots, acc_ref, None, exp_ref, cpl_ref, use_right=False)
    visit(own, plan, ~behind, slots, acc_ref, acc_ref, exp_ref, cpl_ref, use_left=False)


def near_kernel(own_ref, exp_ref, cpl_ref, before_ref, near_ref, acc_ref, near_exp_ref, near_cpl_ref, near_rows_ref, *slots):
    near = near_ref[...]
    prepare(near, near_exp_ref, near_cpl_ref, near_rows_ref)
    place = ((True, 1), (False, 1))
    visit_at(is_second(own_ref), own_ref[...], near, place, acc_ref, before_ref, (exp_ref, cpl_ref), slots)


def gradient(sums, packet_ref):
    return sums[:F] + sums[2 * F :] - packet_ref[:F, :] * sums[F : 2 * F]


def down_kernel(*refs):
    own_ref, exp_ref, cpl_ref, rows_ref, before_ref, near_ref, near_exp_ref, near_cpl_ref, near_rows_ref, down_ref = refs[:10]
    acc_ref, near_grad_ref, back_grad_ref, near_acc_ref, back_ref, *slots = refs[10:]
    second, down = is_second(own_ref), down_ref[...]
    place = ((False, 3), (False, 1))
    back = (back_ref, near_rows_ref, True)
    visit_at(second, near_ref[...], down, place, near_acc_ref, None, (near_exp_ref, near_cpl_ref), slots, back)
    near_grad_ref[...] = gradient(near_acc_ref[...].T, near_ref)
    place = ((False, 2), (False, 2))
    back = (back_ref, rows_ref, False)
    visit_at(second, own_ref[...], down, place, acc_ref, before_ref, (exp_ref, cpl_ref), slots, back)
    back_grad_ref[...] = gradient(back_ref[...], down_ref)


def far_kernel(own_ref, exp_ref, cpl_ref, before_ref, far_ref, more_far_ref, passed_ref, embeddings_ref, grad_ref, acc_ref, *slots):
    far = far_ref[...] + more_far_ref[...]
    visit_at(is_second(own_ref), own_ref[...], far, FAR, acc_ref, before_ref, (exp_ref, cpl_ref), slots)
    grad_ref[...] = gradient(acc_ref[...].T, own_ref) + passed_ref[...]


def last_kernel(grad_ref, back_ref, loglen_ref, embeddings_ref, term_ref):
    grad_z = grad_ref[...] + back_ref[...]
    grad_x = (grad_z * as_column(jnp.exp(-loglen_ref[...]))).astype(jnp.bfloat16)
    for col in range(0, term_ref.shape[1], 512):
        cols = slice(col, col + 512)
        term_ref[:, cols] = jnp.dot(grad_x, embeddings_ref[:, cols], preferred_element_type=jnp.float32)


def as_column(row):
    n = row.shape[1]
    same = lax.broadcasted_iota(jnp.int32, (n, n), 0) == lax.broadcasted_iota(jnp.int32, (n, n), 1)
    return jnp.sum(jnp.where(same, jnp.broadcast_to(row, (n, n)), 0.0), axis=1, keepdims=True)


def project_kernel(plan_ref, projection_ref, loglen_ref, assign_ref, left_ref, right_ref, embeddings_ref, own_ref, *scratch):
    held, sems = scratch[:6], scratch[6]
    points = own_ref.shape[1]
    block = points // PIECES
    sources = (projection_ref, loglen_ref, assign_ref, left_ref, right_ref)
    copies = [pltpu.make_async_copy(source, there, sems.at[n]) for n, (source, there) in enumerate(zip(sources, held))]
    for piece in range(PIECES):
        rows = pl.ds(piece * block, block)
        copies.append(pltpu.make_async_copy(embeddings_ref.at[rows, :], held[5].at[rows, :], sems.at[5 + piece]))
    for copy in copies:
        copy.start()
    for copy in copies[:5]:
        copy.wait()
    projection, loglen, assign, left, right = (there[...] for there in held[:5])
    core = lax.rem(lax.axis_index("blk"), 2).astype(jnp.float32)
    own_ref[LEFT:RIGHT, :] = left
    own_ref[RIGHT:LABEL, :] = right
    rows = [assign.astype(jnp.float32)]
    rows += [jnp.full((1, points), plan_ref[0, offset].astype(jnp.float32)) for offset in range(STEPS)]
    rows += [jnp.full((1, points), core), jnp.zeros((ROWS - CORE - 1, points), jnp.float32)]
    own_ref[LABEL:, :] = jnp.concatenate(rows, axis=0)
    scale = as_column(jnp.exp(-loglen))
    for piece in range(PIECES):
        copies[5 + piece].wait()
        at = slice(piece * block, (piece + 1) * block)
        features = lax.dot_general(held[5][at, :], projection, NT, preferred_element_type=jnp.float32)
        own_ref[:F, at] = features.T * scale


def slots_of(points):
    return [
        pltpu.VMEM((256, points), jnp.bfloat16),
        pltpu.VMEM((256, points), jnp.bfloat16),
        pltpu.VMEM((WIDE, points), jnp.bfloat16),
    ]


def cost(flops, size=4 << 20):
    return pl.CostEstimate(flops=flops, bytes_accessed=size, transcendentals=0)


def project(embeddings, projection, loglen, left_solves, right_solves, assign, plan):
    points = embeddings.shape[0]
    arrays = (projection.T, loglen[None, :], assign[None, :], left_solves, right_solves, embeddings)
    return pl.pallas_call(
        project_kernel,
        in_specs=[pl.BlockSpec(memory_space=pltpu.SMEM)] + [pl.BlockSpec(memory_space=pltpu.HBM)] * len(arrays),
        out_shape=jax.ShapeDtypeStruct((ROWS, points), jnp.float32),
        scratch_shapes=[pltpu.VMEM(array.shape, array.dtype) for array in arrays]
        + [pltpu.SemaphoreType.DMA((5 + PIECES,))],
        cost_estimate=cost(1 << 20),
        compiler_params=pltpu.CompilerParams(vmem_limit_bytes=62 << 20),
        name="project",
    )(plan.T, *arrays)


def tiles(kernel, outs, points, *operands, scratch=()):
    return pl.pallas_call(
        kernel,
        out_shape=outs,
        scratch_shapes=list(scratch) + (slots_of(points) if points else []),
        cost_estimate=cost(1 << 20),
        compiler_params=pltpu.CompilerParams(vmem_limit_bytes=40 << 20),
        name=kernel.__name__,
    )(*operands)


def sent(value, target, takes=lambda source: True):
    count = lax.axis_size("blk")
    pairs = [(source, target(source) % count) for source in range(count) if takes(source)]
    return lax.ppermute(value, "blk", pairs)


def twin(value):
    return sent(value, lambda i: i ^ 1)


def sum_over_blk(term):
    count = lax.axis_size("blk")
    index = lax.axis_index("blk")
    second = (index % 2) == 1
    half = term.shape[0] // 2
    give = jnp.where(second, term[:half], term[half:])
    total = jnp.where(second, term[half:], term[:half]) + twin(give)
    spreads, unit = [], 4
    while unit < count:
        spread = min(4, count // unit)
        place = (index // unit) % spread
        if total.shape[0] % spread == 0:
            spreads.append((unit, spread, place))
            shares = total.reshape(spread, total.shape[0] // spread, total.shape[1])
            total = lax.dynamic_index_in_dim(shares, place, 0, False)
            for hop in range(spread - 1, 0, -1):
                passed = lax.dynamic_index_in_dim(shares, place ^ hop, 0, False)
                total = total + sent(passed, lambda i, step=unit * hop: i ^ step)
        else:
            for bit in range(1, spread.bit_length()):
                total = total + sent(total, lambda i, step=unit * bit: i ^ step)
        unit *= spread
    total = total + sent(total, lambda i: i ^ 2)
    for unit, spread, place in reversed(spreads):
        got = [total] + [sent(total, lambda i, step=unit * hop: i ^ step) for hop in range(1, spread)]
        got = jnp.stack(got)
        total = jnp.concatenate([lax.dynamic_index_in_dim(got, place ^ at, 0, False) for at in range(spread)])
    other = twin(total)
    return jnp.where(second, jnp.concatenate([other, total]), jnp.concatenate([total, other]))


def across(i):
    return i + 3 if i % 2 else i - 3


def per_device(embeddings, projection, loglen, left_solves, right_solves, assign, plan):
    points, width = embeddings.shape
    sums = jax.ShapeDtypeStruct((points, WIDE), jnp.float32)
    factor = jax.ShapeDtypeStruct((points, 256), jnp.bfloat16)
    rows = jax.ShapeDtypeStruct((WIDE, points), jnp.bfloat16)
    block = jax.ShapeDtypeStruct((ROWS, points), jnp.float32)
    grads = jax.ShapeDtypeStruct((F, points), jnp.float32)
    sums_held = pltpu.VMEM(sums.shape, sums.dtype)

    own = project(embeddings, projection, loglen, left_solves, right_solves, assign, plan)
    down = sent(own, lambda i: i + 2)
    far_odd = sent(own, across, lambda i: i // 2 % 2 == 1)
    near = twin(own)
    acc, own_exp, own_cpl, own_rows, own = tiles(home_kernel, (sums, factor, factor, rows, block), points, own)
    far_even = sent(own, across, lambda i: i // 2 % 2 == 0)
    home = (own, own_exp, own_cpl)
    acc, *near_factors = tiles(near_kernel, (sums, factor, factor, rows), points, *home, acc, near)
    acc, near_grad, down_grad = tiles(
        down_kernel,
        (sums, grads, grads),
        points,
        *home,
        own_rows,
        acc,
        near,
        *near_factors,
        down,
        scratch=[sums_held, pltpu.VMEM((WIDE, points), jnp.float32)],
    )
    passed = twin(near_grad)
    back = sent(down_grad, lambda i: i - 2)
    grad = tiles(far_kernel, grads, points, *home, acc, far_odd, far_even, passed, embeddings, scratch=[sums_held])
    term = tiles(
        last_kernel, jax.ShapeDtypeStruct((F, width), jnp.float32), None, grad, back, loglen[None, :], embeddings
    )
    return sum_over_blk(term).T


def solution(mesh):
    return jax.shard_map(
        per_device,
        mesh=mesh,
        in_specs=(
            P(("parts", "blk"), None),
            P("parts", None),
            P("parts"),
            P(None, ("parts", "blk")),
            P(None, ("parts", "blk")),
            P(("parts", "blk")),
            P(None, ("parts", "blk")),
        ),
        out_specs=P("parts", None),
        check_vma=False,
    )
```

time: 95.4 us -> 69.8 us (0.73)
  waiting for transfers between devices: 31 us -> 16.3 us
  matrix products: 6.67 us -> 0 us
  Pallas kernels: 32.7 us -> 27.9 us
  other arithmetic: 3.05 us -> 0.98 us
  starting transfers between devices: 20.3 us -> 21.8 us
  local copies, waits for them, and re-layouts: 1.06 us -> 2.36 us
    ppermute x15, waiting for transfers between devices: 31 us -> 16.3 us  [sent(): return lax.ppermute(value, 'blk', pairs)]
    dot_general x2 -> x0, matrix products: 6.67 us -> none  [the longest x1 3.58 us: project(): lax.dot_general(projection, embeddings, (((0,), (1,)), ((), ())), preferr...]
    pallas_call x5 -> x6, Pallas kernels: 32.7 us -> 27.9 us  [the longest x5 21.4 us: tiles(): pl.pallas_call(kernel, out_shape=outs, scratch_shapes=list(scratch) + (sl...]
    unnamed x16 -> x13, local copies, waits for them, and re-layouts: 0.64 us -> 2.29 us
    ppermute x15, starting transfers between devices: 20.3 us -> 21.8 us  [sent(): return lax.ppermute(value, 'blk', pairs)]
  transfers between devices with their start and end apart: 15 -> 15, of which waited for: 8 -> 10; matrix products, arithmetic and copies ran while one was open for 0% -> 0% of each run, Pallas kernels for 26% -> 28%
where the time goes in v1:
time: 69.8 us; the launch traced here: 69.5 us
  Pallas kernels  27.9 us (40%)
  starting transfers between devices  21.8 us (31%)
  waiting for transfers between devices  16.3 us (23%)
  local copies, waits for them, and re-layouts  2.36 us (3%)
  other arithmetic  0.98 us (1%)
    ppermute x15, starting transfers between devices, sent(): return lax.ppermute(value, 'blk', pairs)  21.8 us
    pallas_call x5, Pallas kernels, tiles(): pl.pallas_call(kernel, out_shape=outs, scratch_shapes=list(scratch) + (sl...  21.4 us
    ppermute x15, waiting for transfers between devices, sent(): return lax.ppermute(value, 'blk', pairs)  16.3 us
    pallas_call x1, Pallas kernels, project(): pl.pallas_call(project_kernel, in_specs=[pl.BlockSpec(memory_space=pltpu....  6.42 us
    unnamed x13, local copies, waits for them, and re-layouts  2.29 us
  transfers between devices with their start and end apart: 15, of which 10 were waited for; matrix products, arithmetic and copies ran while one was open for 0% of the time, Pallas kernels for 28%

profile of v1, /device:TPU:0, one launch (start us, length us, event | category | flops | bytes accessed | tf_op | source)
XLA Modules:
  0.0 69.5 jit_solution(5146325911734977233)
XLA Ops:
  0.0 6.4 %project.1.own_ref = f32[120,1024]{1,0:T(8,128)} custom-call(s32[1,4]{1,0:T(1,128)} %bitcast.44, bf16[64,2048]{1,0:T(8,128)(2,1)} %bitcast.38, f32[1,64]{1,0:T(1,128)} %bitcast.36, s32[1,1024]{1,0:T(1,128)} %bitcast.43, f32[24,1024]{1,0:T(8,128)} %left_ref.1, f32[24,1024]{1,0:T(8,128)} %right_ref.1, bf16[1024,2048]{1,0:T(8,128)(2,1)} %embeddings_ref.5), custom_call_target="tpu_custom_call" | custom-call | flops 1048576 | bytes 4194304 | tf_op jit(solution)/shard_map/project/pallas_call | solution.py:242
  6.4 0.5 collective-permute-start
  6.9 2.6 %collective-permute-start.1 = (f32[120,1024]{1,0:T(8,128)}, f32[120,1024]{1,0:T(8,128)S(1)}, u32[]{:S(2)}, u32[]{:S(2)}) collective-permute-start(f32[120,1024]{1,0:T(8,128)} %project.1.own_ref), channel_id=1, source_target_pairs={{0,2},{1,3},{2,4},{3,5},{4,6},{5,7},{6,8},{7,9},{8,10},{9,11},{10,... | collective-permute-start | bytes 1474568 | tf_op jit(solution)/shard_map/ppermute | solution.py:268
  9.5 5.8 %home_kernel.1 = (f32[1024,192]{1,0:T(8,128)S(1)}, bf16[1024,256]{1,0:T(8,128)(2,1)S(1)}, bf16[1024,256]{1,0:T(8,128)(2,1)S(1)}, bf16[192,1024]{1,0:T(8,128)(2,1)S(1)}, f32[120,1024]{1,0:T(8,128)S(1)}) custom-call(f32[120,1024]{1,0:T(8,128)} %project.1.own_ref), custom_call_target="tpu_custom_call" | custom-call | flops 1048576 | bytes 4194304 | tf_op jit(solution)/shard_map/home_kernel/pallas_call | solution.py:255
  15.3 5.3 %collective-permute-start.3 = (f32[120,1024]{1,0:T(8,128)S(1)}, f32[120,1024]{1,0:T(8,128)S(1)}, u32[]{:S(2)}, u32[]{:S(2)}) collective-permute-start(f32[120,1024]{1,0:T(8,128)S(1)} %get-tuple-element.17.own_ref.refs_0_), channel_id=1, source_target_pairs={{0,13},{1,4},{4,1},{5,8},{8,5},{9,12},{12,9},{13,0},{16,29},{17,20... | collective-permute-start | bytes 1474568 | tf_op jit(solution)/shard_map/ppermute | solution.py:268
  20.6 1.5 %collective-permute-start.2 = (f32[120,1024]{1,0:T(8,128)}, f32[120,1024]{1,0:T(8,128)}, u32[]{:S(2)}, u32[]{:S(2)}) collective-permute-start(f32[120,1024]{1,0:T(8,128)} %project.1.own_ref), channel_id=1, source_target_pairs={{2,15},{3,6},{6,3},{7,10},{10,7},{11,14},{14,11},{15,2},{18,31},{1... | collective-permute-start | bytes 1474568 | tf_op jit(solution)/shard_map/ppermute | solution.py:268
  22.1 0.0 collective-permute-done.near_ref.refs_5_
  22.1 2.5 %near_kernel.1 = (f32[1024,192]{1,0:T(8,128)S(1)}, bf16[1024,256]{1,0:T(8,128)(2,1)S(1)}, bf16[1024,256]{1,0:T(8,128)(2,1)S(1)}, bf16[192,1024]{1,0:T(8,128)(2,1)S(1)}) custom-call(f32[120,1024]{1,0:T(8,128)S(1)} %get-tuple-element.17.own_ref.refs_0_, bf16[1024,256]{1,0:T(8,128)(2,1)S(1)} %get-tuple-element.18.exp_ref.refs_1_, ...), custom_call_target="tpu_custom_call" | custom-call | flops 1048576 | bytes 4194304 | tf_op jit(solution)/shard_map/near_kernel/pallas_call | solution.py:255
  24.6 0.4 collective-permute-done.1.refs_9_
  25.0 7.4 %down_kernel.1 = (f32[1024,192]{1,0:T(8,128)S(1)}, f32[64,1024]{1,0:T(8,128)}, f32[64,1024]{1,0:T(8,128)}) custom-call(f32[120,1024]{1,0:T(8,128)S(1)} %get-tuple-element.17.own_ref.refs_0_, bf16[1024,256]{1,0:T(8,128)(2,1)S(1)} %get-tuple-element.18.exp_ref.refs_1_, bf16[1024,256]{1,0:T(8,128)(2,1)S(1)} %get-tuple-element.19.cpl_ref.refs_2_, ...), custom_call_target="tpu_custom_call" | custom-call | flops 1048576 | bytes 4194304 | tf_op jit(solution)/shard_map/down_kernel/pallas_call | solution.py:255
  32.4 0.0 copy-start.2
  32.4 0.0 collective-permute-start.4
  32.4 1.3 %collective-permute-start.5 = (f32[64,1024]{1,0:T(8,128)}, f32[64,1024]{1,0:T(8,128)}, u32[]{:S(2)}, u32[]{:S(2)}) collective-permute-start(f32[64,1024]{1,0:T(8,128)} %get-tuple-element.28), channel_id=1, source_target_pairs={{0,14},{1,15},{2,0},{3,1},{4,2},{5,3},{6,4},{7,5},{8,6},{9,7},{10,... | collective-permute-start | bytes 786440 | tf_op jit(solution)/shard_map/ppermute | solution.py:268
  33.7 0.0 collective-permute-done.3.more_far_ref
  33.7 0.0 collective-permute-done.2.far_ref
  33.7 0.4 collective-permute-done.4.passed_ref
  34.1 0.0 copy-start
  34.1 2.2 %copy-done = bf16[1024,2048]{1,0:T(8,128)(2,1)S(1)} copy-done((bf16[1024,2048]{1,0:T(8,128)(2,1)S(1)}, bf16[1024,2048]{1,0:T(8,128)(2,1)}, u32[]{:S(2)}) %copy-start) | copy-done | bytes 4194328
  36.3 0.0 copy-start.1
  36.3 3.9 %far_kernel.1.grad_ref = f32[64,1024]{1,0:T(8,128)S(1)} custom-call(f32[120,1024]{1,0:T(8,128)S(1)} %get-tuple-element.17.own_ref.refs_0_, bf16[1024,256]{1,0:T(8,128)(2,1)S(1)} %get-tuple-element.18.exp_ref.refs_1_, bf16[1024,256]{1,0:T(8,128)(2,1)S(1)} %get-tuple-element.19.cpl_ref.refs_2_, f32[1024,192]{1,0:T(8,128)S(1)} %get-tuple-element.26.before_ref, ...), custom_call_target="tpu_custom_call" | custom-call | flops 1048576 | bytes 4194304 | tf_op jit(solution)/shard_map/far_kernel/pallas_call | solution.py:255
  40.2 1.2 %collective-permute-done.5.back_ref = f32[64,1024]{1,0:T(8,128)} collective-permute-done((f32[64,1024]{1,0:T(8,128)}, f32[64,1024]{1,0:T(8,128)}, u32[]{:S(2)}, u32[]{:S(2)}) %collective-permute-start.5) | collective-permute-done | bytes 262176 | tf_op jit(solution)/shard_map/ppermute | solution.py:268
  41.4 0.0 copy-done.2
  41.4 0.0 copy-done.1
  41.4 1.9 %last_kernel.1 = f32[64,2048]{1,0:T(8,128)S(1)} custom-call(f32[64,1024]{1,0:T(8,128)S(1)} %far_kernel.1.grad_ref, f32[64,1024]{1,0:T(8,128)} %collective-permute-done.5.back_ref, f32[1,64]{1,0:T(1,128)S(1)} %bitcast.37, bf16[1024,2048]{1,0:T(8,128)(2,1)S(1)} %copy-done.1), custom_call_target="tpu_custom_call" | custom-call | flops 1048576 | bytes 4194304 | tf_op jit(solution)/shard_map/last_kernel/pallas_call | solution.py:255
  43.3 0.1 collective-permute-start.6
  43.5 1.5 %collective-permute-done.6 = f32[32,2048]{1,0:T(8,128)S(1)} collective-permute-done((f32[32,2048]{1,0:T(8,128)S(1)}, f32[32,2048]{1,0:T(8,128)S(1)}, u32[]{:S(2)}, u32[]{:S(2)}) %collective-permute-start.6) | collective-permute-done | bytes 262176 | tf_op jit(solution)/shard_map/ppermute | solution.py:268
  45.0 1.9 %collective-permute-start.7 = (f32[8,2048]{1,0:T(8,128)S(1)}, f32[8,2048]{1,0:T(8,128)S(1)}, u32[]{:S(2)}, u32[]{:S(2)}) collective-permute-start(f32[8,2048]{1,0:T(8,128)S(1)} %get-tuple-element.39), channel_id=1, source_target_pairs={{0,12},{1,13},{2,14},{3,15},{4,8},{5,9},{6,10},{7,11},{8,4},{9,5},... | collective-permute-start | bytes 196616 | tf_op jit(solution)/shard_map/ppermute | solution.py:268
  46.9 0.0 collective-permute-start.8
  46.9 2.6 %collective-permute-start.9 = (f32[8,2048]{1,0:T(8,128)S(1)}, f32[8,2048]{1,0:T(8,128)S(1)}, u32[]{:S(2)}, u32[]{:S(2)}) collective-permute-start(f32[8,2048]{1,0:T(8,128)S(1)} %get-tuple-element.40), channel_id=1, source_target_pairs={{0,4},{1,5},{2,6},{3,7},{4,0},{5,1},{6,2},{7,3},{8,12},{9,13},{10,... | collective-permute-start | bytes 196616 | tf_op jit(solution)/shard_map/ppermute | solution.py:268
  49.5 2.4 %collective-permute-done.7 = f32[8,2048]{1,0:T(8,128)S(1)} collective-permute-done((f32[8,2048]{1,0:T(8,128)S(1)}, f32[8,2048]{1,0:T(8,128)S(1)}, u32[]{:S(2)}, u32[]{:S(2)}) %collective-permute-start.7) | collective-permute-done | bytes 65568 | tf_op jit(solution)/shard_map/ppermute | solution.py:268
  51.8 2.0 %collective-permute-done.8 = f32[8,2048]{1,0:T(8,128)S(1)} collective-permute-done((f32[8,2048]{1,0:T(8,128)S(1)}, f32[8,2048]{1,0:T(8,128)S(1)}, u32[]{:S(2)}, u32[]{:S(2)}) %collective-permute-start.8) | collective-permute-done | bytes 65568 | tf_op jit(solution)/shard_map/ppermute | solution.py:268
  53.8 0.0 collective-permute-done.9
  53.8 1.6 %collective-permute-start.10 = (f32[8,2048]{1,0:T(8,128)S(1)}, f32[8,2048]{1,0:T(8,128)S(1)}, u32[]{:S(2)}, u32[]{:S(2)}) collective-permute-start(f32[8,2048]{1,0:T(8,128)S(1)} %fusion.1), channel_id=1, source_target_pairs={{0,2},{1,3},{2,0},{3,1},{4,6},{5,7},{6,4},{7,5},{8,10},{9,11},{10,... | collective-permute-start | bytes 196616 | tf_op jit(solution)/shard_map/ppermute | solution.py:268
  55.4 2.8 %collective-permute-done.10 = f32[8,2048]{1,0:T(8,128)S(1)} collective-permute-done((f32[8,2048]{1,0:T(8,128)S(1)}, f32[8,2048]{1,0:T(8,128)S(1)}, u32[]{:S(2)}, u32[]{:S(2)}) %collective-permute-start.10) | collective-permute-done | bytes 65568 | tf_op jit(solution)/shard_map/ppermute | solution.py:268
  58.2 0.9 %collective-permute-start.11 = (f32[8,2048]{1,0:T(8,128)S(1)}, f32[8,2048]{1,0:T(8,128)S(1)}, u32[]{:S(2)}, u32[]{:S(2)}) collective-permute-start(f32[8,2048]{1,0:T(8,128)S(1)} %add.50), channel_id=1, source_target_pairs={{0,4},{1,5},{2,6},{3,7},{4,0},{5,1},{6,2},{7,3},{8,12},{9,13},{10,... | collective-permute-start | bytes 196616 | tf_op jit(solution)/shard_map/ppermute | solution.py:268
  59.1 1.6 %collective-permute-start.12 = (f32[8,2048]{1,0:T(8,128)S(1)}, f32[8,2048]{1,0:T(8,128)S(1)}, u32[]{:S(2)}, u32[]{:S(2)}) collective-permute-start(f32[8,2048]{1,0:T(8,128)S(1)} %add.50), channel_id=1, source_target_pairs={{0,8},{1,9},{2,10},{3,11},{4,12},{5,13},{6,14},{7,15},{8,0},{9,1},... | collective-permute-start | bytes 196616 | tf_op jit(solution)/shard_map/ppermute | solution.py:268
  60.7 1.9 %collective-permute-start.13 = (f32[8,2048]{1,0:T(8,128)S(1)}, f32[8,2048]{1,0:T(8,128)S(1)}, u32[]{:S(2)}, u32[]{:S(2)}) collective-permute-start(f32[8,2048]{1,0:T(8,128)S(1)} %add.50), channel_id=1, source_target_pairs={{0,12},{1,13},{2,14},{3,15},{4,8},{5,9},{6,10},{7,11},{8,4},{9,5},... | collective-permute-start | bytes 196616 | tf_op jit(solution)/shard_map/ppermute | solution.py:268
  62.6 0.0 collective-permute-done.11
  62.6 2.8 %collective-permute-done.12 = f32[8,2048]{1,0:T(8,128)S(1)} collective-permute-done((f32[8,2048]{1,0:T(8,128)S(1)}, f32[8,2048]{1,0:T(8,128)S(1)}, u32[]{:S(2)}, u32[]{:S(2)}) %collective-permute-start.12) | collective-permute-done | bytes 65568 | tf_op jit(solution)/shard_map/ppermute | solution.py:268
  65.4 1.4 %collective-permute-done.13 = f32[8,2048]{1,0:T(8,128)S(1)} collective-permute-done((f32[8,2048]{1,0:T(8,128)S(1)}, f32[8,2048]{1,0:T(8,128)S(1)}, u32[]{:S(2)}, u32[]{:S(2)}) %collective-permute-start.13) | collective-permute-done | bytes 65568 | tf_op jit(solution)/shard_map/ppermute | solution.py:268
  67.0 0.1 collective-permute-start.14
  67.1 1.5 %collective-permute-done.14 = f32[32,2048]{1,0:T(8,128)S(1)} collective-permute-done((f32[32,2048]{1,0:T(8,128)S(1)}, f32[32,2048]{1,0:T(8,128)S(1)}, u32[]{:S(2)}, u32[]{:S(2)}) %collective-permute-start.14) | collective-permute-done | bytes 262176 | tf_op jit(solution)/shard_map/ppermute | solution.py:268
  68.7 0.9 %select_bitcast_fusion = f32[2048,64]{0,1:T(8,128)} fusion(f32[64,2048]{1,0:T(8,128)S(1)} %constant_dynamic-update-slice_fusion, f32[64,2048]{1,0:T(8,128)S(1)} %get-tuple-element.37, pred[]{:T(512)S(6)} %eq.6), kind=kLoop, calls=%fused_computation | loop fusion | flops 131072 | bytes 1572865 | tf_op jit(solution)/shard_map/transpose | solution.py:345
  (16 shorter events, 0.3 us)
Async XLA Ops:
  6.4 15.7 %collective-permute-start = (f32[120,1024]{1,0:T(8,128)}, f32[120,1024]{1,0:T(8,128)S(1)}, u32[]{:S(2)}, u32[]{:S(2)}) collective-permute-start(f32[120,1024]{1,0:T(8,128)} %project.1.own_ref), channel_id=1, source_target_pairs={{0,1},{1,0},{2,3},{3,2},{4,5},{5,4},{6,7},{7,6},{8,9},{9,8},{10,11... | collective-permute-start | bytes 1474568 | tf_op jit(solution)/shard_map/ppermute | solution.py:268
  6.9 18.1 %collective-permute-start.1 = (f32[120,1024]{1,0:T(8,128)}, f32[120,1024]{1,0:T(8,128)S(1)}, u32[]{:S(2)}, u32[]{:S(2)}) collective-permute-start(f32[120,1024]{1,0:T(8,128)} %project.1.own_ref), channel_id=1, source_target_pairs={{0,2},{1,3},{2,4},{3,5},{4,6},{5,7},{6,8},{7,9},{8,10},{9,11},{10,... | collective-permute-start | bytes 1474568 | tf_op jit(solution)/shard_map/ppermute | solution.py:268
  15.3 18.4 %collective-permute-start.3 = (f32[120,1024]{1,0:T(8,128)S(1)}, f32[120,1024]{1,0:T(8,128)S(1)}, u32[]{:S(2)}, u32[]{:S(2)}) collective-permute-start(f32[120,1024]{1,0:T(8,128)S(1)} %get-tuple-element.17.own_ref.refs_0_), channel_id=1, source_target_pairs={{0,13},{1,4},{4,1},{5,8},{8,5},{9,12},{12,9},{13,0},{16,29},{17,20... | collective-permute-start | bytes 1474568 | tf_op jit(solution)/shard_map/ppermute | solution.py:268
  20.6 13.1 %collective-permute-start.2 = (f32[120,1024]{1,0:T(8,128)}, f32[120,1024]{1,0:T(8,128)}, u32[]{:S(2)}, u32[]{:S(2)}) collective-permute-start(f32[120,1024]{1,0:T(8,128)} %project.1.own_ref), channel_id=1, source_target_pairs={{2,15},{3,6},{6,3},{7,10},{10,7},{11,14},{14,11},{15,2},{18,31},{1... | collective-permute-start | bytes 1474568 | tf_op jit(solution)/shard_map/ppermute | solution.py:268
  32.4 9.0 %copy-start.2 = (f32[64]{0:T(128)S(1)}, f32[64]{0:T(128)}, u32[]{:S(2)}) copy-start(f32[64]{0:T(128)} %param.9) | copy-start | bytes 772
  32.4 1.7 %collective-permute-start.4 = (f32[64,1024]{1,0:T(8,128)}, f32[64,1024]{1,0:T(8,128)S(1)}, u32[]{:S(2)}, u32[]{:S(2)}) collective-permute-start(f32[64,1024]{1,0:T(8,128)} %get-tuple-element.27), channel_id=1, source_target_pairs={{0,1},{1,0},{2,3},{3,2},{4,5},{5,4},{6,7},{7,6},{8,9},{9,8},{10,11... | collective-permute-start | bytes 786440 | tf_op jit(solution)/shard_map/ppermute | solution.py:268
  32.4 9.0 %collective-permute-start.5 = (f32[64,1024]{1,0:T(8,128)}, f32[64,1024]{1,0:T(8,128)}, u32[]{:S(2)}, u32[]{:S(2)}) collective-permute-start(f32[64,1024]{1,0:T(8,128)} %get-tuple-element.28), channel_id=1, source_target_pairs={{0,14},{1,15},{2,0},{3,1},{4,2},{5,3},{6,4},{7,5},{8,6},{9,7},{10,... | collective-permute-start | bytes 786440 | tf_op jit(solution)/shard_map/ppermute | solution.py:268
  34.1 2.2 %copy-start = (bf16[1024,2048]{1,0:T(8,128)(2,1)S(1)}, bf16[1024,2048]{1,0:T(8,128)(2,1)}, u32[]{:S(2)}) copy-start(bf16[1024,2048]{1,0:T(8,128)(2,1)} %embeddings_ref.5) | copy-start | bytes 12582916
  36.3 5.1 %copy-start.1 = (bf16[1024,2048]{1,0:T(8,128)(2,1)S(1)}, bf16[1024,2048]{1,0:T(8,128)(2,1)}, u32[]{:S(2)}) copy-start(bf16[1024,2048]{1,0:T(8,128)(2,1)} %embeddings_ref.5) | copy-start | bytes 12582916
  43.3 1.6 %collective-permute-start.6 = (f32[32,2048]{1,0:T(8,128)S(1)}, f32[32,2048]{1,0:T(8,128)S(1)}, u32[]{:S(2)}, u32[]{:S(2)}) collective-permute-start(f32[32,2048]{1,0:T(8,128)S(1)} %slice_select_fusion), channel_id=1, source_target_pairs={{0,1},{1,0},{2,3},{3,2},{4,5},{5,4},{6,7},{7,6},{8,9},{9,8},{10,11... | collective-permute-start | bytes 786440 | tf_op jit(solution)/shard_map/ppermute | solution.py:268
  45.0 6.8 %collective-permute-start.7 = (f32[8,2048]{1,0:T(8,128)S(1)}, f32[8,2048]{1,0:T(8,128)S(1)}, u32[]{:S(2)}, u32[]{:S(2)}) collective-permute-start(f32[8,2048]{1,0:T(8,128)S(1)} %get-tuple-element.39), channel_id=1, source_target_pairs={{0,12},{1,13},{2,14},{3,15},{4,8},{5,9},{6,10},{7,11},{8,4},{9,5},... | collective-permute-start | bytes 196616 | tf_op jit(solution)/shard_map/ppermute | solution.py:268
  46.9 6.9 %collective-permute-start.8 = (f32[8,2048]{1,0:T(8,128)S(1)}, f32[8,2048]{1,0:T(8,128)S(1)}, u32[]{:S(2)}, u32[]{:S(2)}) collective-permute-start(f32[8,2048]{1,0:T(8,128)S(1)} %get-tuple-element.41), channel_id=1, source_target_pairs={{0,8},{1,9},{2,10},{3,11},{4,12},{5,13},{6,14},{7,15},{8,0},{9,1},... | collective-permute-start | bytes 196616 | tf_op jit(solution)/shard_map/ppermute | solution.py:268
  46.9 6.9 %collective-permute-start.9 = (f32[8,2048]{1,0:T(8,128)S(1)}, f32[8,2048]{1,0:T(8,128)S(1)}, u32[]{:S(2)}, u32[]{:S(2)}) collective-permute-start(f32[8,2048]{1,0:T(8,128)S(1)} %get-tuple-element.40), channel_id=1, source_target_pairs={{0,4},{1,5},{2,6},{3,7},{4,0},{5,1},{6,2},{7,3},{8,12},{9,13},{10,... | collective-permute-start | bytes 196616 | tf_op jit(solution)/shard_map/ppermute | solution.py:268
  53.8 4.3 %collective-permute-start.10 = (f32[8,2048]{1,0:T(8,128)S(1)}, f32[8,2048]{1,0:T(8,128)S(1)}, u32[]{:S(2)}, u32[]{:S(2)}) collective-permute-start(f32[8,2048]{1,0:T(8,128)S(1)} %fusion.1), channel_id=1, source_target_pairs={{0,2},{1,3},{2,0},{3,1},{4,6},{5,7},{6,4},{7,5},{8,10},{9,11},{10,... | collective-permute-start | bytes 196616 | tf_op jit(solution)/shard_map/ppermute | solution.py:268
  58.2 4.5 %collective-permute-start.11 = (f32[8,2048]{1,0:T(8,128)S(1)}, f32[8,2048]{1,0:T(8,128)S(1)}, u32[]{:S(2)}, u32[]{:S(2)}) collective-permute-start(f32[8,2048]{1,0:T(8,128)S(1)} %add.50), channel_id=1, source_target_pairs={{0,4},{1,5},{2,6},{3,7},{4,0},{5,1},{6,2},{7,3},{8,12},{9,13},{10,... | collective-permute-start | bytes 196616 | tf_op jit(solution)/shard_map/ppermute | solution.py:268
  59.1 6.3 %collective-permute-start.12 = (f32[8,2048]{1,0:T(8,128)S(1)}, f32[8,2048]{1,0:T(8,128)S(1)}, u32[]{:S(2)}, u32[]{:S(2)}) collective-permute-start(f32[8,2048]{1,0:T(8,128)S(1)} %add.50), channel_id=1, source_target_pairs={{0,8},{1,9},{2,10},{3,11},{4,12},{5,13},{6,14},{7,15},{8,0},{9,1},... | collective-permute-start | bytes 196616 | tf_op jit(solution)/shard_map/ppermute | solution.py:268
  60.7 6.1 %collective-permute-start.13 = (f32[8,2048]{1,0:T(8,128)S(1)}, f32[8,2048]{1,0:T(8,128)S(1)}, u32[]{:S(2)}, u32[]{:S(2)}) collective-permute-start(f32[8,2048]{1,0:T(8,128)S(1)} %add.50), channel_id=1, source_target_pairs={{0,12},{1,13},{2,14},{3,15},{4,8},{5,9},{6,10},{7,11},{8,4},{9,5},... | collective-permute-start | bytes 196616 | tf_op jit(solution)/shard_map/ppermute | solution.py:268
  67.0 1.6 %collective-permute-start.14 = (f32[32,2048]{1,0:T(8,128)S(1)}, f32[32,2048]{1,0:T(8,128)S(1)}, u32[]{:S(2)}, u32[]{:S(2)}) collective-permute-start(f32[32,2048]{1,0:T(8,128)S(1)} %pad_maximum_fusion.1), channel_id=1, source_target_pairs={{0,1},{1,0},{2,3},{3,2},{4,5},{5,4},{6,7},{7,6},{8,9},{9,8},{10,11... | collective-permute-start | bytes 786440 | tf_op jit(solution)/shard_map/ppermute | solution.py:268

commit v2 on v1

--- a/solution.py
+++ b/solution.py
@@ -22,7 +22,7 @@
 LOG2E = 1.4426950408889634
 OFF = -1e30
 CHUNK = 512
-PIECES = 8
+PIECES = 2
 WIDE = 3 * F
 FAR = ((False, 3), (True, 3))
 NT = (((1,), (1,)), ((), ()))
@@ -84,8 +84,15 @@
     return exponent.astype(jnp.bfloat16), coupling.astype(jnp.bfloat16), grads.astype(jnp.bfloat16)
 
 
-def add_tile(acc_ref, before_ref, home_exp_ref, home_cpl_ref, slots, back=None):
-    exp_ref, cpl_ref, grad_ref = slots
+def weights_of(home_exp, home_cpl, exp_ref, cpl_ref, cols):
+    power = jnp.dot(home_exp, exp_ref[:, cols], preferred_element_type=jnp.float32)
+    couple = jnp.dot(home_cpl, cpl_ref[:, cols], preferred_element_type=jnp.float32)
+    weights = jnp.exp2(power) * couple
+    hi = weights.astype(jnp.bfloat16)
+    return hi, (weights - hi.astype(jnp.float32)).astype(jnp.bfloat16)
+
+
+def add_tile(acc_ref, before_ref, home_exp_ref, home_cpl_ref, exp_ref, cpl_ref, grad_ref):
     points, visitors = home_exp_ref.shape[0], exp_ref.shape[1]
     for row in range(0, points, CHUNK):
         rows = slice(row, row + CHUNK)
@@ -93,40 +100,65 @@
         total = None if before_ref is None else before_ref[rows, :]
         for col in range(0, visitors, CHUNK):
             cols = slice(col, col + CHUNK)
-            power = jnp.dot(home_exp, exp_ref[:, cols], preferred_element_type=jnp.float32)
-            couple = jnp.dot(home_cpl, cpl_ref[:, cols], preferred_element_type=jnp.float32)
-            weights = jnp.exp2(power) * couple
-            hi = weights.astype(jnp.bfloat16)
-            lo = (weights - hi.astype(jnp.float32)).astype(jnp.bfloat16)
-            for part in (hi, lo):
+            for part in weights_of(home_exp, home_cpl, exp_ref, cpl_ref, cols):
                 term = lax.dot_general(part, grad_ref[:, cols], NT, preferred_element_type=jnp.float32)
                 total = term if total is None else total + term
-            if back is not None:
-                back_ref, home_rows_ref, fresh = back
-                term = jnp.dot(home_rows_ref[:, rows], hi, preferred_element_type=jnp.float32)
-                term += jnp.dot(home_rows_ref[:, rows], lo, preferred_element_type=jnp.float32)
-                back_ref[:, cols] = term if fresh and row == 0 else back_ref[:, cols] + term
         acc_ref[rows, :] = total
 
 
-def visit(packet, plan, ahead, slots, acc_ref, before_ref, home_exp_ref, home_cpl_ref, back=None, **uses):
+def back_tile(back_ref, fresh, home_exp_ref, home_cpl_ref, home_rows_ref, exp_ref, cpl_ref, hi_ref, lo_ref):
+    points, visitors = home_exp_ref.shape[0], exp_ref.shape[1]
+    for row in range(0, points, CHUNK):
+        rows = slice(row, row + CHUNK)
+        home_exp, home_cpl, home_rows = home_exp_ref[rows, :], home_cpl_ref[rows, :], home_rows_ref[:, rows]
+        for col in range(0, visitors, CHUNK):
+            cols = slice(col, col + CHUNK)
+            hi, lo = weights_of(home_exp, home_cpl, exp_ref, cpl_ref, cols)
+            hi_ref[rows, cols], lo_ref[rows, cols] = hi, lo
+            term = jnp.dot(home_rows, hi, preferred_element_type=jnp.float32)
+            term += jnp.dot(home_rows, lo, preferred_element_type=jnp.float32)
+            back_ref[:, cols] = term if fresh and row == 0 else back_ref[:, cols] + term
+
+
+def side_tile(acc_ref, before_ref, hi_ref, lo_ref, grad_ref):
+    points, visitors = hi_ref.shape
+    for row in range(0, points, CHUNK):
+        rows = slice(row, row + CHUNK)
+        total = None if before_ref is None else before_ref[rows, :]
+        for col in range(0, visitors, CHUNK):
+            cols = slice(col, col + CHUNK)
+            for part in (hi_ref[rows, cols], lo_ref[rows, cols]):
+                term = lax.dot_general(part, grad_ref[:, cols], NT, preferred_element_type=jnp.float32)
+                total = term if total is None else total + term
+        acc_ref[rows, :] = total
+
+
+def load(slots, packet, plan, ahead, **uses):
     exp_ref, cpl_ref, grad_ref = slots
     bias = bias_rows(plan, packet[LABEL : LABEL + 1].astype(jnp.int32), ahead)
     exp_ref[...], cpl_ref[...], grad_ref[...] = visitor_operands(packet, bias, **uses)
-    add_tile(acc_ref, before_ref, home_exp_ref, home_cpl_ref, slots, back)
+
+
+def visit(packet, plan, ahead, slots, acc_ref, before_ref, home_exp_ref, home_cpl_ref, **uses):
+    load(slots, packet, plan, ahead, **uses)
+    add_tile(acc_ref, before_ref, home_exp_ref, home_cpl_ref, *slots)
 
 
 def plan_of(packet, offset):
     return packet[PLAN + offset : PLAN + offset + 1].astype(jnp.int32)
 
 
-def visit_at(second, home, packet, place, acc_ref, before_ref, factors, slots, back=None):
+def load_at(slots, second, home, packet, place):
     (ahead_first, offset_first), (ahead_second, offset_second) = place
     ahead = jnp.logical_or(jnp.logical_and(second, ahead_second), jnp.logical_and(~second, ahead_first))
     mine = jnp.where(second, plan_of(home, offset_second), plan_of(home, offset_first))
     theirs = jnp.where(second, plan_of(packet, offset_second), plan_of(packet, offset_first))
-    plan = jnp.where(ahead, theirs, mine)
-    visit(packet, plan, ahead, slots, acc_ref, before_ref, *factors, back=back)
+    load(slots, packet, jnp.where(ahead, theirs, mine), ahead)
+
+
+def visit_at(second, home, packet, place, acc_ref, before_ref, factors, slots):
+    load_at(slots, second, home, packet, place)
+    add_tile(acc_ref, before_ref, *factors, *slots)
 
 
 def prepare(packet, exp_ref, cpl_ref, rows_ref):
@@ -162,31 +194,30 @@
 
 
 def down_kernel(*refs):
-    own_ref, exp_ref, cpl_ref, rows_ref, before_ref, near_ref, near_exp_ref, near_cpl_ref, near_rows_ref, down_ref = refs[:10]
-    acc_ref, near_grad_ref, back_grad_ref, near_acc_ref, back_ref, *slots = refs[10:]
+    own_ref, exp_ref, cpl_ref, rows_ref, near_ref, near_exp_ref, near_cpl_ref, near_rows_ref, down_ref = refs[:9]
+    hi_ref, lo_ref, near_hi_ref, near_lo_ref, grad_rows_ref, back_grad_ref, turn_ref, back_ref, *slots = refs[9:]
     second, down = is_second(own_ref), down_ref[...]
-    place = ((False, 3), (False, 1))
-    back = (back_ref, near_rows_ref, True)
-    visit_at(second, near_ref[...], down, place, near_acc_ref, None, (near_exp_ref, near_cpl_ref), slots, back)
+    load_at(slots, second, near_ref[...], down, ((False, 3), (False, 1)))
+    back_tile(back_ref, True, near_exp_ref, near_cpl_ref, near_rows_ref, slots[0], slots[1], near_hi_ref, near_lo_ref)
+    load_at(slots, second, own_ref[...], down, ((False, 2), (False, 2)))
+    back_tile(back_ref, False, exp_ref, cpl_ref, rows_ref, slots[0], slots[1], hi_ref, lo_ref)
+    back_grad_ref[...] = gradient(back_ref[...], down_ref)
+    turn_ref[...] = back_grad_ref[:8, :128]
+    grad_rows_ref[...] = slots[2][...]
+
+
+def side_kernel(*refs):
+    before_ref, near_ref, hi_ref, lo_ref, near_hi_ref, near_lo_ref, grad_rows_ref, _, acc_ref, near_grad_ref, near_acc_ref = refs
+    side_tile(near_acc_ref, None, near_hi_ref, near_lo_ref, grad_rows_ref)
     near_grad_ref[...] = gradient(near_acc_ref[...].T, near_ref)
-    place = ((False, 2), (False, 2))
-    back = (back_ref, rows_ref, False)
-    visit_at(second, own_ref[...], down, place, acc_ref, before_ref, (exp_ref, cpl_ref), slots, back)
-    back_grad_ref[...] = gradient(back_ref[...], down_ref)
-
-
-def far_kernel(own_ref, exp_ref, cpl_ref, before_ref, far_ref, more_far_ref, passed_ref, embeddings_ref, grad_ref, acc_ref, *slots):
-    far = far_ref[...] + more_far_ref[...]
+    side_tile(acc_ref, before_ref, hi_ref, lo_ref, grad_rows_ref)
+
+
+def far_kernel(own_ref, exp_ref, cpl_ref, before_ref, far_ref, loglen_ref, grad_ref, scale_ref, acc_ref, *slots):
+    scale_ref[...] = jnp.broadcast_to(as_column(jnp.exp(-loglen_ref[...])), scale_ref.shape)
+    far = far_ref[...]
     visit_at(is_second(own_ref), own_ref[...], far, FAR, acc_ref, before_ref, (exp_ref, cpl_ref), slots)
-    grad_ref[...] = gradient(acc_ref[...].T, own_ref) + passed_ref[...]
-
-
-def last_kernel(grad_ref, back_ref, loglen_ref, embeddings_ref, term_ref):
-    grad_z = grad_ref[...] + back_ref[...]
-    grad_x = (grad_z * as_column(jnp.exp(-loglen_ref[...]))).astype(jnp.bfloat16)
-    for col in range(0, term_ref.shape[1], 512):
-        cols = slice(col, col + 512)
-        term_ref[:, cols] = jnp.dot(grad_x, embeddings_ref[:, cols], preferred_element_type=jnp.float32)
+    grad_ref[...] = gradient(acc_ref[...].T, own_ref)
 
 
 def as_column(row):
@@ -220,8 +251,8 @@
     for piece in range(PIECES):
         copies[5 + piece].wait()
         at = slice(piece * block, (piece + 1) * block)
-        features = lax.dot_general(held[5][at, :], projection, NT, preferred_element_type=jnp.float32)
-        own_ref[:F, at] = features.T * scale
+        features = lax.dot_general(projection, held[5][at, :], NT, preferred_element_type=jnp.float32)
+        own_ref[:F, at] = features * scale
 
 
 def slots_of(points):
@@ -308,7 +339,7 @@
 
 
 def per_device(embeddings, projection, loglen, left_solves, right_solves, assign, plan):
-    points, width = embeddings.shape
+    points = embeddings.shape[0]
     sums = jax.ShapeDtypeStruct((points, WIDE), jnp.float32)
     factor = jax.ShapeDtypeStruct((points, 256), jnp.bfloat16)
     rows = jax.ShapeDtypeStruct((WIDE, points), jnp.bfloat16)
@@ -318,30 +349,29 @@
 
     own = project(embeddings, projection, loglen, left_solves, right_solves, assign, plan)
     down = sent(own, lambda i: i + 2)
-    far_odd = sent(own, across, lambda i: i // 2 % 2 == 1)
     near = twin(own)
     acc, own_exp, own_cpl, own_rows, own = tiles(home_kernel, (sums, factor, factor, rows, block), points, own)
-    far_even = sent(own, across, lambda i: i // 2 % 2 == 0)
+    far = sent(own, across)
     home = (own, own_exp, own_cpl)
     acc, *near_factors = tiles(near_kernel, (sums, factor, factor, rows), points, *home, acc, near)
-    acc, near_grad, down_grad = tiles(
+    weights = jax.ShapeDtypeStruct((points, points), jnp.bfloat16)
+    *kept, down_rows, down_grad, turn = tiles(
         down_kernel,
-        (sums, grads, grads),
+        (weights, weights, weights, weights, rows, grads, jax.ShapeDtypeStruct((8, 128), jnp.float32)),
         points,
         *home,
         own_rows,
-        acc,
         near,
         *near_factors,
         down,
-        scratch=[sums_held, pltpu.VMEM((WIDE, points), jnp.float32)],
+        scratch=[pltpu.VMEM((WIDE, points), jnp.float32)],
     )
+    back = sent(down_grad, lambda i: i - 2)
+    acc, near_grad = tiles(side_kernel, (sums, grads), None, acc, near, *kept, down_rows, twin(turn), scratch=[sums_held])
     passed = twin(near_grad)
-    back = sent(down_grad, lambda i: i - 2)
-    grad = tiles(far_kernel, grads, points, *home, acc, far_odd, far_even, passed, embeddings, scratch=[sums_held])
-    term = tiles(
-        last_kernel, jax.ShapeDtypeStruct((F, width), jnp.float32), None, grad, back, loglen[None, :], embeddings
-    )
+    grad, scale = tiles(far_kernel, (grads, grads), points, *home, acc, far, loglen[None, :], scratch=[sums_held])
+    grad_x = ((grad + passed + back) * scale).astype(jnp.bfloat16)
+    term = lax.dot_general(grad_x, embeddings, (((1,), (0,)), ((), ())), preferred_element_type=jnp.float32)
     return sum_over_blk(term).T
 
 

time: 69.8 us -> 66.7 us (0.956)
  Pallas kernels: 27.9 us -> 23 us
  matrix products: 0 us -> 3.18 us
  starting transfers between devices: 21.8 us -> 19.9 us
  waiting for transfers between devices: 16.3 us -> 17.9 us
  local copies, waits for them, and re-layouts: 2.36 us -> 1.23 us
    pallas_call x5, Pallas kernels: 21.4 us -> 18.2 us  [tiles(): pl.pallas_call(kernel, out_shape=outs, scratch_shapes=list(scratch) + (sl...]
    dot_general x0 -> x1, matrix products: none -> 3.18 us  [per_device(): lax.dot_general(grad_x, embeddings, (((1,), (0,)), ((), ())), preferred_e...]
    ppermute x15, starting transfers between devices: 21.8 us -> 19.9 us  [sent(): return lax.ppermute(value, 'blk', pairs)]
    ppermute x15, waiting for transfers between devices: 16.3 us -> 17.9 us  [sent(): return lax.ppermute(value, 'blk', pairs)]
    pallas_call x1, Pallas kernels: 6.42 us -> 4.84 us  [project(): pl.pallas_call(project_kernel, in_specs=[pl.BlockSpec(memory_space=pltpu....]
    unnamed x13 -> x11, local copies, waits for them, and re-layouts: 2.29 us -> 1.16 us
  transfers between devices with their start and end apart: 15 -> 15, of which waited for: 10 -> 9; matrix products, arithmetic and copies ran while one was open for 0% -> 0% of each run, Pallas kernels for 28% -> 27%
where the time goes in v2:
time: 66.7 us; the launch traced here: 66.5 us
  Pallas kernels  23 us (34%)
  starting transfers between devices  19.9 us (30%)
  waiting for transfers between devices  17.9 us (27%)
  matrix products  3.18 us (5%)
  local copies, waits for them, and re-layouts  1.23 us (2%)
  other arithmetic  0.99 us (1%)
    ppermute x15, starting transfers between devices, sent(): return lax.ppermute(value, 'blk', pairs)  19.9 us
    pallas_call x5, Pallas kernels, tiles(): pl.pallas_call(kernel, out_shape=outs, scratch_shapes=list(scratch) + (sl...  18.2 us
    ppermute x15, waiting for transfers between devices, sent(): return lax.ppermute(value, 'blk', pairs)  17.9 us
    pallas_call x1, Pallas kernels, project(): pl.pallas_call(project_kernel, in_specs=[pl.BlockSpec(memory_space=pltpu....  4.84 us
    dot_general x1, matrix products, per_device(): lax.dot_general(grad_x, embeddings, (((1,), (0,)), ((), ())), preferred_e...  3.18 us
  transfers between devices with their start and end apart: 15, of which 9 were waited for; matrix products, arithmetic and copies ran while one was open for 0% of the time, Pallas kernels for 27%

profile of v2, /device:TPU:0, one launch (start us, length us, event | category | flops | bytes accessed | tf_op | source)
XLA Modules:
  0.0 66.5 jit_solution(10384755931910914933)
XLA Ops:
  0.0 4.8 %project.1.own_ref = f32[120,1024]{1,0:T(8,128)} custom-call(s32[1,4]{1,0:T(1,128)} %bitcast.45, bf16[64,2048]{1,0:T(8,128)(2,1)} %bitcast.39, f32[1,64]{1,0:T(1,128)} %bitcast.37, s32[1,1024]{1,0:T(1,128)} %bitcast.44, f32[24,1024]{1,0:T(8,128)} %left_ref.1, f32[24,1024]{1,0:T(8,128)} %right_ref.1, bf16[1024,2048]{1,0:T(8,128)(2,1)} %embeddings_ref.1), custom_call_target="tpu_custom_call" | custom-call | flops 1048576 | bytes 4194304 | tf_op jit(solution)/shard_map/project/pallas_call | solution.py:273
  4.8 0.5 collective-permute-start
  5.4 2.6 %collective-permute-start.1 = (f32[120,1024]{1,0:T(8,128)}, f32[120,1024]{1,0:T(8,128)S(1)}, u32[]{:S(2)}, u32[]{:S(2)}) collective-permute-start(f32[120,1024]{1,0:T(8,128)} %project.1.own_ref), channel_id=1, source_target_pairs={{0,2},{1,3},{2,4},{3,5},{4,6},{5,7},{6,8},{7,9},{8,10},{9,11},{10,... | collective-permute-start | bytes 1474568 | tf_op jit(solution)/shard_map/ppermute | solution.py:299
  7.9 0.0 copy-start
  7.9 1.1 %copy-done = f32[120,1024]{1,0:T(8,128)S(1)} copy-done((f32[120,1024]{1,0:T(8,128)S(1)}, f32[120,1024]{1,0:T(8,128)}, u32[]{:S(2)}) %copy-start) | copy-done | bytes 491544
  9.0 4.7 %home_kernel.1 = (f32[1024,192]{1,0:T(8,128)S(1)}, bf16[1024,256]{1,0:T(8,128)(2,1)S(1)}, bf16[1024,256]{1,0:T(8,128)(2,1)S(1)}, bf16[192,1024]{1,0:T(8,128)(2,1)S(1)}, f32[120,1024]{1,0:T(8,128)S(1)}) custom-call(f32[120,1024]{1,0:T(8,128)S(1)} %copy-done), custom_call_target="tpu_custom_call" | custom-call | flops 1048576 | bytes 4194304 | tf_op jit(solution)/shard_map/home_kernel/pallas_call | solution.py:286
  13.7 3.4 %collective-permute-start.3 = (f32[120,1024]{1,0:T(8,128)S(1)}, f32[120,1024]{1,0:T(8,128)S(1)}, u32[]{:S(2)}, u32[]{:S(2)}) collective-permute-start(f32[120,1024]{1,0:T(8,128)S(1)} %get-tuple-element.25.own_ref.refs_0_), channel_id=1, source_target_pairs={{0,13},{1,4},{2,15},{3,6},{4,1},{5,8},{6,3},{7,10},{8,5},{9,12},{1... | collective-permute-start | bytes 1474568 | tf_op jit(solution)/shard_map/ppermute | solution.py:299
  17.2 0.0 collective-permute-done.near_ref.refs_4_.refs_1_
  17.2 2.5 %near_kernel.1 = (f32[1024,192]{1,0:T(8,128)S(1)}, bf16[1024,256]{1,0:T(8,128)(2,1)S(1)}, bf16[1024,256]{1,0:T(8,128)(2,1)S(1)}, bf16[192,1024]{1,0:T(8,128)(2,1)S(1)}) custom-call(f32[120,1024]{1,0:T(8,128)S(1)} %get-tuple-element.25.own_ref.refs_0_, bf16[1024,256]{1,0:T(8,128)(2,1)S(1)} %get-tuple-element.26.exp_ref.refs_1_, ...), custom_call_target="tpu_custom_call" | custom-call | flops 1048576 | bytes 4194304 | tf_op jit(solution)/shard_map/near_kernel/pallas_call | solution.py:286
  19.7 3.7 %collective-permute-done.1.refs_8_ = f32[120,1024]{1,0:T(8,128)S(1)} collective-permute-done((f32[120,1024]{1,0:T(8,128)}, f32[120,1024]{1,0:T(8,128)S(1)}, u32[]{:S(2)}, u32[]{:S(2)}) %collective-permute-start.1) | collective-permute-done | bytes 491552 | tf_op jit(solution)/shard_map/ppermute | solution.py:299
  23.4 5.2 %down_kernel.1 = (bf16[1024,1024]{1,0:T(8,128)(2,1)S(1)}, bf16[1024,1024]{1,0:T(8,128)(2,1)S(1)}, bf16[1024,1024]{1,0:T(8,128)(2,1)S(1)}, bf16[1024,1024]{1,0:T(...) custom-call(f32[120,1024]{1,0:T(8,128)S(1)} %get-tuple-element.25.own_ref.refs_0_, ...), custom_call_target="tpu_custom_call" | custom-call | flops 1048576 | bytes 4194304 | tf_op jit(solution)/shard_map/down_kernel/pallas_call | solution.py:286
  28.6 0.1 collective-permute-start.2
  28.7 1.6 %collective-permute-start.5 = (f32[64,1024]{1,0:T(8,128)S(1)}, f32[64,1024]{1,0:T(8,128)}, u32[]{:S(2)}, u32[]{:S(2)}) collective-permute-start(f32[64,1024]{1,0:T(8,128)S(1)} %get-tuple-element.43), channel_id=1, source_target_pairs={{0,14},{1,15},{2,0},{3,1},{4,2},{5,3},{6,4},{7,5},{8,6},{9,7},{10,... | collective-permute-start | bytes 786440 | tf_op jit(solution)/shard_map/ppermute | solution.py:299
  30.3 0.0 collective-permute-done.2.refs_7_
  30.3 0.0 copy-start.1
  30.3 3.0 %side_kernel.1 = (f32[1024,192]{1,0:T(8,128)S(1)}, f32[64,1024]{1,0:T(8,128)}) custom-call(f32[1024,192]{1,0:T(8,128)S(1)} %get-tuple-element.29.refs_0_, f32[120,1024]{1,0:T(8,128)S(1)} %collective-permute-done.near_ref.refs_4_.refs_1_, bf16[1024,1024]{1,0:T(8,128)(2,1)S(1)} %get-tuple-element.34.refs_2_, bf16[1024,1024]{1,0:T(8,128)(2,1)S(1)} %get-tuple-element.35.refs_3_, ...), custom_call_target="tpu_custom_call" | custom-call | flops 1048576 | bytes 4194304 | tf_op jit(solution)/shard_map/side_kernel/pallas_call | solution.py:286
  33.3 0.0 collective-permute-start.4
  33.3 0.0 collective-permute-done.3.far_ref
  33.3 0.0 copy-done.1
  33.3 2.7 %far_kernel.1 = (f32[64,1024]{1,0:T(8,128)S(1)}, f32[64,1024]{1,0:T(8,128)S(1)}) custom-call(f32[120,1024]{1,0:T(8,128)S(1)} %get-tuple-element.25.own_ref.refs_0_, bf16[1024,256]{1,0:T(8,128)(2,1)S(1)} %get-tuple-element.26.exp_ref.refs_1_, bf16[1024,256]{1,0:T(8,128)(2,1)S(1)} %get-tuple-element.27.cpl_ref.refs_2_, ...), custom_call_target="tpu_custom_call" | custom-call | flops 1048576 | bytes 4194304 | tf_op jit(solution)/shard_map/far_kernel/pallas_call | solution.py:286
  36.0 1.5 %collective-permute-done.5 = f32[64,1024]{1,0:T(8,128)} collective-permute-done((f32[64,1024]{1,0:T(8,128)S(1)}, f32[64,1024]{1,0:T(8,128)}, u32[]{:S(2)}, u32[]{:S(2)}) %collective-permute-start.5) | collective-permute-done | bytes 262176 | tf_op jit(solution)/shard_map/ppermute | solution.py:299
  37.5 0.0 collective-permute-done.4
  37.5 3.2 %fusion = f32[64,2048]{1,0:T(8,128)S(1)} fusion(bf16[1024,2048]{1,0:T(8,128)(2,1)} %embeddings_ref.1, f32[64,1024]{1,0:T(8,128)S(1)} %get-tuple-element.44, f32[64,1024]{1,0:T(8,128)} %collective-permute-done.5, f32[64,1024]{1,0:T(8,128)S(1)} %get-tuple-element.41, f32[64,1024]{1,0:T(8,128)} %collective-permute-done.4), kind=kOutput, calls=%fused_computation.6 | convolution fusion | flops 268697600 | bytes 5767168 | tf_op jit(solution)/shard_map/dot_general | solution.py:374
  40.7 0.1 collective-permute-start.6
  40.9 1.5 %collective-permute-done.6 = f32[32,2048]{1,0:T(8,128)S(1)} collective-permute-done((f32[32,2048]{1,0:T(8,128)S(1)}, f32[32,2048]{1,0:T(8,128)S(1)}, u32[]{:S(2)}, u32[]{:S(2)}) %collective-permute-start.6) | collective-permute-done | bytes 262176 | tf_op jit(solution)/shard_map/ppermute | solution.py:299
  42.4 0.1 collective-permute-start.9
  42.5 2.5 %collective-permute-start.8 = (f32[8,2048]{1,0:T(8,128)S(1)}, f32[8,2048]{1,0:T(8,128)S(1)}, u32[]{:S(2)}, u32[]{:S(2)}) collective-permute-start(f32[8,2048]{1,0:T(8,128)S(1)} %get-tuple-element.57), channel_id=1, source_target_pairs={{0,8},{1,9},{2,10},{3,11},{4,12},{5,13},{6,14},{7,15},{8,0},{9,1},... | collective-permute-start | bytes 196616 | tf_op jit(solution)/shard_map/ppermute | solution.py:299
  45.0 1.9 %collective-permute-start.7 = (f32[8,2048]{1,0:T(8,128)S(1)}, f32[8,2048]{1,0:T(8,128)S(1)}, u32[]{:S(2)}, u32[]{:S(2)}) collective-permute-start(f32[8,2048]{1,0:T(8,128)S(1)} %get-tuple-element.55), channel_id=1, source_target_pairs={{0,12},{1,13},{2,14},{3,15},{4,8},{5,9},{6,10},{7,11},{8,4},{9,5},... | collective-permute-start | bytes 196616 | tf_op jit(solution)/shard_map/ppermute | solution.py:299
  46.9 0.8 %collective-permute-done.9 = f32[8,2048]{1,0:T(8,128)S(1)} collective-permute-done((f32[8,2048]{1,0:T(8,128)S(1)}, f32[8,2048]{1,0:T(8,128)S(1)}, u32[]{:S(2)}, u32[]{:S(2)}) %collective-permute-start.9) | collective-permute-done | bytes 65568 | tf_op jit(solution)/shard_map/ppermute | solution.py:299
  47.6 3.5 %collective-permute-done.8 = f32[8,2048]{1,0:T(8,128)S(1)} collective-permute-done((f32[8,2048]{1,0:T(8,128)S(1)}, f32[8,2048]{1,0:T(8,128)S(1)}, u32[]{:S(2)}, u32[]{:S(2)}) %collective-permute-start.8) | collective-permute-done | bytes 65568 | tf_op jit(solution)/shard_map/ppermute | solution.py:299
  51.2 0.0 collective-permute-done.7
  51.2 2.7 %collective-permute-start.10 = (f32[8,2048]{1,0:T(8,128)S(1)}, f32[8,2048]{1,0:T(8,128)S(1)}, u32[]{:S(2)}, u32[]{:S(2)}) collective-permute-start(f32[8,2048]{1,0:T(8,128)S(1)} %fusion.2), channel_id=1, source_target_pairs={{0,2},{1,3},{2,0},{3,1},{4,6},{5,7},{6,4},{7,5},{8,10},{9,11},{10,... | collective-permute-start | bytes 196616 | tf_op jit(solution)/shard_map/ppermute | solution.py:299
  53.9 2.2 %collective-permute-done.10 = f32[8,2048]{1,0:T(8,128)S(1)} collective-permute-done((f32[8,2048]{1,0:T(8,128)S(1)}, f32[8,2048]{1,0:T(8,128)S(1)}, u32[]{:S(2)}, u32[]{:S(2)}) %collective-permute-start.10) | collective-permute-done | bytes 65568 | tf_op jit(solution)/shard_map/ppermute | solution.py:299
  56.2 2.0 %collective-permute-start.13 = (f32[8,2048]{1,0:T(8,128)S(1)}, f32[8,2048]{1,0:T(8,128)S(1)}, u32[]{:S(2)}, u32[]{:S(2)}) collective-permute-start(f32[8,2048]{1,0:T(8,128)S(1)} %add.58), channel_id=1, source_target_pairs={{0,12},{1,13},{2,14},{3,15},{4,8},{5,9},{6,10},{7,11},{8,4},{9,5},... | collective-permute-start | bytes 196616 | tf_op jit(solution)/shard_map/ppermute | solution.py:299
  58.1 0.3 collective-permute-start.12
  58.4 2.2 %collective-permute-start.11 = (f32[8,2048]{1,0:T(8,128)S(1)}, f32[8,2048]{1,0:T(8,128)S(1)}, u32[]{:S(2)}, u32[]{:S(2)}) collective-permute-start(f32[8,2048]{1,0:T(8,128)S(1)} %add.58), channel_id=1, source_target_pairs={{0,4},{1,5},{2,6},{3,7},{4,0},{5,1},{6,2},{7,3},{8,12},{9,13},{10,... | collective-permute-start | bytes 196616 | tf_op jit(solution)/shard_map/ppermute | solution.py:299
  60.6 1.7 %collective-permute-done.13 = f32[8,2048]{1,0:T(8,128)S(1)} collective-permute-done((f32[8,2048]{1,0:T(8,128)S(1)}, f32[8,2048]{1,0:T(8,128)S(1)}, u32[]{:S(2)}, u32[]{:S(2)}) %collective-permute-start.13) | collective-permute-done | bytes 65568 | tf_op jit(solution)/shard_map/ppermute | solution.py:299
  62.3 1.5 %collective-permute-done.12 = f32[8,2048]{1,0:T(8,128)S(1)} collective-permute-done((f32[8,2048]{1,0:T(8,128)S(1)}, f32[8,2048]{1,0:T(8,128)S(1)}, u32[]{:S(2)}, u32[]{:S(2)}) %collective-permute-start.12) | collective-permute-done | bytes 65568 | tf_op jit(solution)/shard_map/ppermute | solution.py:299
  63.8 0.0 collective-permute-done.11
  63.9 0.1 collective-permute-start.14
  64.0 1.5 %collective-permute-done.14 = f32[32,2048]{1,0:T(8,128)S(1)} collective-permute-done((f32[32,2048]{1,0:T(8,128)S(1)}, f32[32,2048]{1,0:T(8,128)S(1)}, u32[]{:S(2)}, u32[]{:S(2)}) %collective-permute-start.14) | collective-permute-done | bytes 262176 | tf_op jit(solution)/shard_map/ppermute | solution.py:299
  65.6 0.9 %select_bitcast_fusion = f32[2048,64]{0,1:T(8,128)} fusion(f32[64,2048]{1,0:T(8,128)S(1)} %constant_dynamic-update-slice_fusion, f32[64,2048]{1,0:T(8,128)S(1)} %get-tuple-element.53, pred[]{:T(512)S(6)} %eq.6), kind=kLoop, calls=%fused_computation | loop fusion | flops 131072 | bytes 1572865 | tf_op jit(solution)/shard_map/transpose | solution.py:375
  (16 shorter events, 0.3 us)
Async XLA Ops:
  4.8 12.3 %collective-permute-start = (f32[120,1024]{1,0:T(8,128)}, f32[120,1024]{1,0:T(8,128)S(1)}, u32[]{:S(2)}, u32[]{:S(2)}) collective-permute-start(f32[120,1024]{1,0:T(8,128)} %project.1.own_ref), channel_id=1, source_target_pairs={{0,1},{1,0},{2,3},{3,2},{4,5},{5,4},{6,7},{7,6},{8,9},{9,8},{10,11... | collective-permute-start | bytes 1474568 | tf_op jit(solution)/shard_map/ppermute | solution.py:299
  5.4 18.1 %collective-permute-start.1 = (f32[120,1024]{1,0:T(8,128)}, f32[120,1024]{1,0:T(8,128)S(1)}, u32[]{:S(2)}, u32[]{:S(2)}) collective-permute-start(f32[120,1024]{1,0:T(8,128)} %project.1.own_ref), channel_id=1, source_target_pairs={{0,2},{1,3},{2,4},{3,5},{4,6},{5,7},{6,8},{7,9},{8,10},{9,11},{10,... | collective-permute-start | bytes 1474568 | tf_op jit(solution)/shard_map/ppermute | solution.py:299
  7.9 1.1 %copy-start = (f32[120,1024]{1,0:T(8,128)S(1)}, f32[120,1024]{1,0:T(8,128)}, u32[]{:S(2)}) copy-start(f32[120,1024]{1,0:T(8,128)} %project.1.own_ref) | copy-start | bytes 1474564
  13.7 19.6 %collective-permute-start.3 = (f32[120,1024]{1,0:T(8,128)S(1)}, f32[120,1024]{1,0:T(8,128)S(1)}, u32[]{:S(2)}, u32[]{:S(2)}) collective-permute-start(f32[120,1024]{1,0:T(8,128)S(1)} %get-tuple-element.25.own_ref.refs_0_), channel_id=1, source_target_pairs={{0,13},{1,4},{2,15},{3,6},{4,1},{5,8},{6,3},{7,10},{8,5},{9,12},{1... | collective-permute-start | bytes 1474568 | tf_op jit(solution)/shard_map/ppermute | solution.py:299
  28.6 1.7 %collective-permute-start.2 = (f32[8,128]{1,0:T(8,128)S(1)}, f32[8,128]{1,0:T(8,128)S(1)}, u32[]{:S(2)}, u32[]{:S(2)}) collective-permute-start(f32[8,128]{1,0:T(8,128)S(1)} %get-tuple-element.39), channel_id=1, source_target_pairs={{0,1},{1,0},{2,3},{3,2},{4,5},{5,4},{6,7},{7,6},{8,9},{9,8},{10,11... | collective-permute-start | bytes 12296 | tf_op jit(solution)/shard_map/ppermute | solution.py:299
  28.7 8.8 %collective-permute-start.5 = (f32[64,1024]{1,0:T(8,128)S(1)}, f32[64,1024]{1,0:T(8,128)}, u32[]{:S(2)}, u32[]{:S(2)}) collective-permute-start(f32[64,1024]{1,0:T(8,128)S(1)} %get-tuple-element.43), channel_id=1, source_target_pairs={{0,14},{1,15},{2,0},{3,1},{4,2},{5,3},{6,4},{7,5},{8,6},{9,7},{10,... | collective-permute-start | bytes 786440 | tf_op jit(solution)/shard_map/ppermute | solution.py:299
  30.3 3.0 %copy-start.1 = (f32[64]{0:T(128)S(1)}, f32[64]{0:T(128)}, u32[]{:S(2)}) copy-start(f32[64]{0:T(128)} %param.9) | copy-start | bytes 772
  33.3 4.2 %collective-permute-start.4 = (f32[64,1024]{1,0:T(8,128)}, f32[64,1024]{1,0:T(8,128)}, u32[]{:S(2)}, u32[]{:S(2)}) collective-permute-start(f32[64,1024]{1,0:T(8,128)} %get-tuple-element.42), channel_id=1, source_target_pairs={{0,1},{1,0},{2,3},{3,2},{4,5},{5,4},{6,7},{7,6},{8,9},{9,8},{10,11... | collective-permute-start | bytes 786440 | tf_op jit(solution)/shard_map/ppermute | solution.py:299
  40.7 1.6 %collective-permute-start.6 = (f32[32,2048]{1,0:T(8,128)S(1)}, f32[32,2048]{1,0:T(8,128)S(1)}, u32[]{:S(2)}, u32[]{:S(2)}) collective-permute-start(f32[32,2048]{1,0:T(8,128)S(1)} %slice_select_fusion), channel_id=1, source_target_pairs={{0,1},{1,0},{2,3},{3,2},{4,5},{5,4},{6,7},{7,6},{8,9},{9,8},{10,11... | collective-permute-start | bytes 786440 | tf_op jit(solution)/shard_map/ppermute | solution.py:299
  42.4 5.2 %collective-permute-start.9 = (f32[8,2048]{1,0:T(8,128)S(1)}, f32[8,2048]{1,0:T(8,128)S(1)}, u32[]{:S(2)}, u32[]{:S(2)}) collective-permute-start(f32[8,2048]{1,0:T(8,128)S(1)} %get-tuple-element.56), channel_id=1, source_target_pairs={{0,4},{1,5},{2,6},{3,7},{4,0},{5,1},{6,2},{7,3},{8,12},{9,13},{10,... | collective-permute-start | bytes 196616 | tf_op jit(solution)/shard_map/ppermute | solution.py:299
  42.5 8.7 %collective-permute-start.8 = (f32[8,2048]{1,0:T(8,128)S(1)}, f32[8,2048]{1,0:T(8,128)S(1)}, u32[]{:S(2)}, u32[]{:S(2)}) collective-permute-start(f32[8,2048]{1,0:T(8,128)S(1)} %get-tuple-element.57), channel_id=1, source_target_pairs={{0,8},{1,9},{2,10},{3,11},{4,12},{5,13},{6,14},{7,15},{8,0},{9,1},... | collective-permute-start | bytes 196616 | tf_op jit(solution)/shard_map/ppermute | solution.py:299
  45.0 6.2 %collective-permute-start.7 = (f32[8,2048]{1,0:T(8,128)S(1)}, f32[8,2048]{1,0:T(8,128)S(1)}, u32[]{:S(2)}, u32[]{:S(2)}) collective-permute-start(f32[8,2048]{1,0:T(8,128)S(1)} %get-tuple-element.55), channel_id=1, source_target_pairs={{0,12},{1,13},{2,14},{3,15},{4,8},{5,9},{6,10},{7,11},{8,4},{9,5},... | collective-permute-start | bytes 196616 | tf_op jit(solution)/shard_map/ppermute | solution.py:299
  51.2 5.0 %collective-permute-start.10 = (f32[8,2048]{1,0:T(8,128)S(1)}, f32[8,2048]{1,0:T(8,128)S(1)}, u32[]{:S(2)}, u32[]{:S(2)}) collective-permute-start(f32[8,2048]{1,0:T(8,128)S(1)} %fusion.2), channel_id=1, source_target_pairs={{0,2},{1,3},{2,0},{3,1},{4,6},{5,7},{6,4},{7,5},{8,10},{9,11},{10,... | collective-permute-start | bytes 196616 | tf_op jit(solution)/shard_map/ppermute | solution.py:299
  56.2 6.1 %collective-permute-start.13 = (f32[8,2048]{1,0:T(8,128)S(1)}, f32[8,2048]{1,0:T(8,128)S(1)}, u32[]{:S(2)}, u32[]{:S(2)}) collective-permute-start(f32[8,2048]{1,0:T(8,128)S(1)} %add.58), channel_id=1, source_target_pairs={{0,12},{1,13},{2,14},{3,15},{4,8},{5,9},{6,10},{7,11},{8,4},{9,5},... | collective-permute-start | bytes 196616 | tf_op jit(solution)/shard_map/ppermute | solution.py:299
  58.1 5.7 %collective-permute-start.12 = (f32[8,2048]{1,0:T(8,128)S(1)}, f32[8,2048]{1,0:T(8,128)S(1)}, u32[]{:S(2)}, u32[]{:S(2)}) collective-permute-start(f32[8,2048]{1,0:T(8,128)S(1)} %add.58), channel_id=1, source_target_pairs={{0,8},{1,9},{2,10},{3,11},{4,12},{5,13},{6,14},{7,15},{8,0},{9,1},... | collective-permute-start | bytes 196616 | tf_op jit(solution)/shard_map/ppermute | solution.py:299
  58.4 5.3 %collective-permute-start.11 = (f32[8,2048]{1,0:T(8,128)S(1)}, f32[8,2048]{1,0:T(8,128)S(1)}, u32[]{:S(2)}, u32[]{:S(2)}) collective-permute-start(f32[8,2048]{1,0:T(8,128)S(1)} %add.58), channel_id=1, source_target_pairs={{0,4},{1,5},{2,6},{3,7},{4,0},{5,1},{6,2},{7,3},{8,12},{9,13},{10,... | collective-permute-start | bytes 196616 | tf_op jit(solution)/shard_map/ppermute | solution.py:299
  63.9 1.6 %collective-permute-start.14 = (f32[32,2048]{1,0:T(8,128)S(1)}, f32[32,2048]{1,0:T(8,128)S(1)}, u32[]{:S(2)}, u32[]{:S(2)}) collective-permute-start(f32[32,2048]{1,0:T(8,128)S(1)} %pad_maximum_fusion.1), channel_id=1, source_target_pairs={{0,1},{1,0},{2,3},{3,2},{4,5},{5,4},{6,7},{7,6},{8,9},{9,8},{10,11... | collective-permute-start | bytes 786440 | tf_op jit(solution)/shard_map/ppermute | solution.py:299
